TPU v7x, 32 devices: a whole 2x2x4 slice. The times are simulated.
32 devices in a mesh: dp: 8 (over z, y), mp: 4 (over x, core).
Axes of the slice: x: 2, y: 2, z: 4, core: 2. Of those that a mesh axis runs over, the one named last changes fastest.
Arguments:
- tokens: bfloat16 [2048, 2048], P('dp'), may hold values from -6 to 6
- lengths: int32 [4], replicated, may hold values from 1 to 1024, 2048 in all
- w_query: float32 [2048, 2048], P('dp', 'mp')
- w_key: float32 [2048, 2048], P('dp', 'mp')
- w_value: float32 [2048, 2048], P('dp', 'mp'), may hold values from -0.125 to 0.125
- w_out: float32 [2048, 2048], P('dp', 'mp'), may hold values from -0.125 to 0.125
- w_gate: float32 [2048, 4096], P('dp', 'mp'), may hold values from -0.125 to 0.125
- w_up: float32 [2048, 4096], P('dp', 'mp'), may hold values from -0.125 to 0.125
- w_down: float32 [4096, 2048], P('dp', 'mp'), may hold values from -0.09375 to 0.09375
Outputs:
- layer_out: bfloat16 [2048, 2048], P(('dp', 'mp'))
Inputs may be any that keep to these rules, and one draw needn't show every extreme that they name: Every prompt is 1 to 1024 tokens long and one is exactly 1024; the lengths sum to 2048.
All inputs are finite; a program needn't handle non-finite values.
Results may differ from a plain program's by a relative error of at most 0.02.
The roundings to bfloat16 on the way count: a program that leaves them out, or rounds other values in their place, can miss the bound.
Values may be sent and summed in bfloat16 or wider, within the bound.
A program may use at most 128 MiB of HBM per device.

v0:
```python
import jax
import jax.numpy as jnp
from jax import lax
from jax.sharding import PartitionSpec as P

HEAD = 128


epsilon = 1e-05
theta_base = 10000.0


def passed_along(value, axis, steps):
    count = lax.axis_size(axis)
    initial, last = (max(0, -steps), min(count, count - steps))
    return lax.ppermute(value, axis, [(source, source + steps) for source in range(initial, last)])


def layer_norm(rows):
    values = rows.astype(jnp.float32)
    centre = jnp.mean(values, axis=-1, keepdims=True)
    spread = jnp.mean(jnp.square(values - centre), axis=-1, keepdims=True)
    return (values - centre) * lax.rsqrt(spread + epsilon)


def prompt_coords(first, count, lengths):
    where = first + jnp.arange(count)
    ends = jnp.cumsum(lengths)
    passed = (ends[None, :] <= where[:, None]).astype(jnp.int32)
    prompt = jnp.sum(passed, axis=1)
    offset = where - jnp.sum(passed * lengths[None, :], axis=1)
    prompt = jnp.where(where < 0, -1, prompt)
    return (prompt, offset, where)


def rotate(values, offset):
    half = values.shape[-1] // 2
    freqs = jnp.power(theta_base, -jnp.arange(half, dtype=jnp.float32) * 2.0 / values.shape[-1])
    angles = offset.astype(jnp.float32)[:, None] * freqs[None, :]
    cosine = jnp.cos(angles)[:, None, :]
    sine = jnp.sin(angles)[:, None, :]
    first_half = values[..., :half]
    second_half = values[..., half:]
    return jnp.concatenate(
        [first_half * cosine - second_half * sine, second_half * cosine + first_half * sine],
        axis=-1,
    )


def row_product(left, pieces):
    block = jnp.concatenate(pieces, axis=1)
    return jnp.dot(left, block, preferred_element_type=jnp.float32)


def on_device(tokens, lengths, w_query, w_key, w_value, w_out, w_gate, w_up, w_down):
    half_type = jnp.bfloat16
    rows = tokens.shape[0]
    narrow = w_query.shape[1]
    heads_dev = narrow // HEAD
    dp_index = lax.axis_index("dp")
    mp_index = lax.axis_index("mp")
    reach = lax.axis_size("dp") // 2
    normed = layer_norm(tokens).astype(half_type)
    joined = row_product(
        normed,
        (
            lax.all_gather(w_query.astype(half_type), "dp", axis=0, tiled=True),
            lax.all_gather(w_key.astype(half_type), "dp", axis=0, tiled=True),
            lax.all_gather(w_value.astype(half_type), "dp", axis=0, tiled=True),
        ),
    )
    q_prompt, q_offset, q_where = prompt_coords(dp_index * rows, rows, lengths)
    shaped = joined.reshape(rows, 3, heads_dev, HEAD)
    query = rotate(shaped[:, 0], q_offset).astype(half_type)
    keys = rotate(shaped[:, 1], q_offset).astype(half_type)
    values = shaped[:, 2].astype(half_type)
    own_first = dp_index * rows
    own_pair = jnp.stack((keys, values))
    scale = 1.0 / HEAD**0.5

    def online_step(state, pair, first):
        accum, total, top = state
        k_prompt, k_offset, k_where = prompt_coords(first, rows, lengths)
        scores = (
            jnp.einsum("qhd,khd->hqk", query, pair[0], preferred_element_type=jnp.float32) * scale
        )
        allowed = (q_prompt[:, None] == k_prompt[None, :]) & (k_where[None, :] <= q_where[:, None])
        scores = jnp.where(allowed[None], scores, -jnp.inf)
        new_top = jnp.maximum(top, jnp.max(scores, axis=-1, keepdims=True))
        fade = jnp.exp(top - new_top)
        weights = jnp.exp(scores - new_top)
        probs = weights.astype(half_type)
        product = jnp.einsum("hqk,khd->qhd", probs, pair[1], preferred_element_type=jnp.float32)
        accum = accum * jnp.transpose(fade, (1, 0, 2)) + product
        total = total * fade + jnp.sum(weights, axis=-1, keepdims=True)
        return (accum, total, new_top)

    start_state = (
        jnp.zeros((rows, heads_dev, HEAD), jnp.float32),
        jnp.zeros((heads_dev, rows, 1), jnp.float32),
        jnp.full((heads_dev, rows, 1), -jnp.inf, jnp.float32),
    )
    state = online_step(start_state, own_pair, own_first)

    def relay_step(hop, carry):
        carried, running = carry
        carried = passed_along(carried, "dp", 1)
        first = own_first - (hop + 1) * rows
        return (carried, online_step(running, carried, first))

    unused, state = lax.fori_loop(0, reach, relay_step, (own_pair, state))
    accum, total, top = state
    context = (accum / jnp.transpose(total, (1, 0, 2))).astype(half_type).reshape(rows, narrow)
    by_rows = lax.all_gather(w_out.astype(half_type), "dp", axis=0, tiled=True)
    server_out = lax.all_to_all(by_rows, "mp", split_axis=0, concat_axis=1, tiled=True)
    partial_out = jnp.dot(context, server_out, preferred_element_type=jnp.float32)
    attended = lax.psum(partial_out.astype(jnp.bfloat16), "mp").astype(jnp.float32)
    mixed = (tokens.astype(jnp.float32) + attended).astype(half_type)
    normed_two = layer_norm(mixed).astype(half_type)
    units = w_gate.shape[1]
    gate_up = row_product(
        normed_two,
        (
            lax.all_gather(w_gate.astype(half_type), "dp", axis=0, tiled=True),
            lax.all_gather(w_up.astype(half_type), "dp", axis=0, tiled=True),
        ),
    )
    hidden = (jax.nn.silu(gate_up[:, :units]) * gate_up[:, units:]).astype(half_type)
    gathered_down = lax.all_gather(w_down.astype(half_type), "dp", axis=0, tiled=True)
    slab = rows // lax.axis_size("mp")
    server_down = lax.all_to_all(gathered_down, "mp", split_axis=0, concat_axis=1, tiled=True)
    share = lax.psum_scatter(
        jnp.dot(hidden, server_down, preferred_element_type=jnp.float32).astype(jnp.bfloat16),
        "mp",
        scatter_dimension=0,
        tiled=True,
    ).astype(jnp.float32)
    own_rows = lax.dynamic_slice_in_dim(mixed, mp_index * slab, slab, 0)
    return (own_rows.astype(jnp.float32) + share).astype(half_type)


def solution(mesh):
    in_specs = (
        P("dp", None),
        P(),
        P("dp", "mp"),
        P("dp", "mp"),
        P("dp", "mp"),
        P("dp", "mp"),
        P("dp", "mp"),
        P("dp", "mp"),
        P("dp", "mp"),
    )
    out_specs = P(("dp", "mp"), None)
    return jax.shard_map(
        on_device, mesh=mesh, in_specs=in_specs, out_specs=out_specs, check_vma=False
    )
```

profile of v0, /device:TPU:9, one launch (start us, length us, event | category | flops | bytes accessed | tf_op | source)
XLA Modules:
  0.0 581.2 jit_solution(2651095963052008917)
XLA Ops:
  6.5 1.9 convert_element_type.122
  8.5 1.8 convert_element_type.123
  10.4 0.7 convert_element_type.121
  11.2 0.7 convert_element_type.131
  12.0 0.9 convert_element_type.141
  13.4 0.4 fusion.23
  14.1 0.5 multiply_cosine_fusion
  14.6 44.5 %all-gather.10.cloned.1.call-done = bf16[2048,512]{1,0:T(8,128)(2,1)} async-done(((bf16[256,512]{1,0:T(8,128)(2,1)}), bf16[2048,512]{1,0:T(8,128)(2,1)}) %all-gather.10.cloned.1.call-update) | async-done | bytes 2097168 | tf_op jit(solution)/shard_map/all_gather | solution.py:68
  59.1 49.9 %all-gather.12.cloned.1.call-done = bf16[2048,512]{1,0:T(8,128)(2,1)} async-done(((bf16[256,512]{1,0:T(8,128)(2,1)}), bf16[2048,512]{1,0:T(8,128)(2,1)}) %all-gather.12.cloned.1.call-update) | async-done | bytes 2097168 | tf_op jit(solution)/shard_map/all_gather | solution.py:69
  109.1 49.9 %all-gather.8.cloned.1.call-done = bf16[2048,512]{1,0:T(8,128)(2,1)} async-done(((bf16[256,512]{1,0:T(8,128)(2,1)}), bf16[2048,512]{1,0:T(8,128)(2,1)}) %all-gather.8.cloned.1.call-update) | async-done | bytes 2097168 | tf_op jit(solution)/shard_map/all_gather | solution.py:67
  159.0 5.2 fusion.13
  164.2 1.8 reshape.337
  166.4 0.4 subtract_convert_fusion
  167.0 0.4 fusion.58
  167.6 0.3 fusion.29
  168.1 40.7 %all-gather.14.cloned.1.call-done = bf16[2048,512]{1,0:T(8,128)(2,1)} async-done(((bf16[256,512]{1,0:T(8,128)(2,1)}), bf16[2048,512]{1,0:T(8,128)(2,1)}) %all-gather.14.cloned.1.call-update) | async-done | bytes 2097168 | tf_op jit(solution)/shard_map/all_gather | solution.py:114
  208.8 5.9 %all-to-all-start = ((bf16[4,512,512]{2,1,0:T(8,128)(2,1)}), bf16[4,512,512]{2,1,0:T(8,128)(2,1)}, u32[]{:S(2)}, u32[]{:S(2)}) async-start(bf16[4,512,512]{2,1,0:T(8,128)(2,1)} %bitcast.88), calls=%async_computation | async-start | bytes 4194304 | tf_op jit(solution)/shard_map/all_to_all | solution.py:115
  214.9 100.3 %while.23 = (s32[]{:T(128)}, bf16[2,256,4,128]{3,1,2,0:T(8,128)(2,1)S(1)}, f32[256,4,128]{2,0,1:T(8,128)S(1)}, f32[4,256,1]{1,0,2:T(4,128)S(1)}, f32[4,256,1]{1,...) while((s32[]{:T(128)}, ...), condition=%wide.region_11.12_spmd.clone.clone, body=%wide.region_7.11_spmd.clone.clone.sunk | while | flops 136518656 | bytes 8333513 | solution.py:111
  214.9 2.2 collective-permute-start
  217.4 23.5 %collective-permute-done = bf16[2,256,4,128]{3,1,2,0:T(8,128)(2,1)S(1)} collective-permute-done((bf16[2,256,4,128]{3,1,2,0:T(8,128)(2,1)S(1)}, bf16[2,256,4,128]{3,1,2,0:T(8,128)(2,1)S(1)}, u32[]{:S(2)}, u32[]{:S(2)}) %collective-permute-start) | collective-permute-done | bytes 524320 | tf_op jit(solution)/shard_map/while/body/eval_jaxpr/ppermute | solution.py:16
  240.9 0.3 fusion.72
  241.5 0.5 fusion.74
  241.9 3.4 collective-permute-start
  245.6 15.8 %collective-permute-done = bf16[2,256,4,128]{3,1,2,0:T(8,128)(2,1)S(1)} collective-permute-done((bf16[2,256,4,128]{3,1,2,0:T(8,128)(2,1)S(1)}, bf16[2,256,4,128]{3,1,2,0:T(8,128)(2,1)S(1)}, u32[]{:S(2)}, u32[]{:S(2)}) %collective-permute-start) | collective-permute-done | bytes 524320 | tf_op jit(solution)/shard_map/while/body/eval_jaxpr/ppermute | solution.py:16
  261.4 0.3 fusion.72
  262.0 0.5 fusion.74
  262.4 2.5 collective-permute-start
  265.2 23.6 %collective-permute-done = bf16[2,256,4,128]{3,1,2,0:T(8,128)(2,1)S(1)} collective-permute-done((bf16[2,256,4,128]{3,1,2,0:T(8,128)(2,1)S(1)}, bf16[2,256,4,128]{3,1,2,0:T(8,128)(2,1)S(1)}, u32[]{:S(2)}, u32[]{:S(2)}) %collective-permute-start) | collective-permute-done | bytes 524320 | tf_op jit(solution)/shard_map/while/body/eval_jaxpr/ppermute | solution.py:16
  288.8 0.3 fusion.72
  289.4 0.5 fusion.74
  289.9 1.9 collective-permute-start
  292.0 22.1 %collective-permute-done = bf16[2,256,4,128]{3,1,2,0:T(8,128)(2,1)S(1)} collective-permute-done((bf16[2,256,4,128]{3,1,2,0:T(8,128)(2,1)S(1)}, bf16[2,256,4,128]{3,1,2,0:T(8,128)(2,1)S(1)}, u32[]{:S(2)}, u32[]{:S(2)}) %collective-permute-start) | collective-permute-done | bytes 524320 | tf_op jit(solution)/shard_map/while/body/eval_jaxpr/ppermute | solution.py:16
  314.7 0.5 fusion.74
  315.4 2.8 copy.43
  318.2 1.8 convolution_convert_fusion
  320.1 2.2 convert_element_type.138
  322.4 0.9 convert_element_type.139
  323.3 12.2 %all-to-all-start.1 = ((bf16[4,1024,512]{2,1,0:T(8,128)(2,1)}), bf16[4,1024,512]{2,1,0:T(8,128)(2,1)}, u32[]{:S(2)}, u32[]{:S(2)}) async-start(bf16[4,1024,512]{2,1,0:T(8,128)(2,1)} %bitcast.82), calls=%async_computation.1 | async-start | bytes 8388608 | tf_op jit(solution)/shard_map/all_to_all | solution.py:131
  335.5 46.0 %all-reduce.2.cloned.1.call-done = bf16[256,2048]{1,0:T(8,128)(2,1)} async-done(((bf16[256,2048]{1,0:T(8,128)(2,1)}), bf16[256,2048]{1,0:T(8,128)(2,1)}) %all-reduce.2.cloned.1.call-update) | async-done | bytes 1048592 | tf_op jit(solution)/shard_map/psum | solution.py:117
  381.5 1.6 convert_reduce_fusion.2
  383.1 0.4 fusion.25
  383.5 71.9 %all-gather.16.cloned.1.call-done = bf16[2048,1024]{1,0:T(8,128)(2,1)} async-done(((bf16[256,1024]{1,0:T(8,128)(2,1)}), bf16[2048,1024]{1,0:T(8,128)(2,1)}) %all-gather.16.cloned.1.call-update) | async-done | bytes 4194320 | tf_op jit(solution)/shard_map/all_gather | solution.py:124
  455.4 74.0 %all-gather.18.cloned.1.call-done = bf16[2048,1024]{1,0:T(8,128)(2,1)} async-done(((bf16[256,1024]{1,0:T(8,128)(2,1)}), bf16[2048,1024]{1,0:T(8,128)(2,1)}) %all-gather.18.cloned.1.call-update) | async-done | bytes 4194320 | tf_op jit(solution)/shard_map/all_gather | solution.py:125
  529.4 7.2 %fusion.9 = f32[256,2048]{1,0:T(8,128)} fusion(bf16[2048,1024]{1,0:T(8,128)(2,1)} %all-gather.18.cloned.1.call-done, bf16[2048,1024]{1,0:T(8,128)(2,1)} %all-gather.16.cloned.1.call-done, bf16[256,2048]{1,0:T(8,128)(2,1)S(1)} %get-tuple-element.345, f32[256]{0:T(256)S(1)} %add_rsqrt_fusion, f32[256]{0:T(256)S(1)} %broadcast_multiply_fusion), kind=kOutput, calls=%fused_computation.20 | convolution fusion | flops 2166358016 | bytes 11536384 | tf_op jit(solution)/shard_map/dot_general | solution.py:52
  536.6 6.3 %copy.44 = bf16[1024,4,512]{0,2,1:T(8,128)(2,1)} copy(bf16[1024,4,512]{2,0,1:T(8,128)(2,1)} %bitcast.20) | data formatting | bytes 8388608 | tf_op jit(solution)/shard_map/all_to_all | solution.py:131
  542.9 5.1 convolution_convert_fusion.1
  548.0 25.0 %reduce-scatter.2.cloned.1.call-done = bf16[64,2048]{1,0:T(8,128)(2,1)} async-done(((bf16[256,2048]{1,0:T(8,128)(2,1)}), bf16[64,2048]{1,0:T(8,128)(2,1)}) %reduce-scatter.2.cloned.1.call-update) | async-done | bytes 262160 | tf_op jit(solution)/shard_map/reduce_scatter | solution.py:132
  573.0 1.7 add_convert_fusion
  (92 shorter events, 4.6 us)
Async XLA Ops:
  6.5 3.9 copy-start.3
  6.5 4.7 copy-start.4
  6.5 5.5 copy-start.1
  6.5 52.6 %all-gather.10.cloned.1.call-start = ((), (), s32[]{:S(2)}) async-start(), calls=%async_computation.4 | async-start | bytes 2359296 | tf_op jit(solution)/shard_map/all_gather | solution.py:68
  8.5 100.6 %all-gather.12.cloned.1.call-start = ((), (), s32[]{:S(2)}) async-start(), calls=%async_computation.5 | async-start | bytes 2359296 | tf_op jit(solution)/shard_map/all_gather | solution.py:69
  10.3 2.7 copy-start.5
  10.3 2.8 copy-start
  10.4 148.6 %all-gather.8.cloned.1.call-start = ((), (), s32[]{:S(2)}) async-start(), calls=%async_computation.3 | async-start | bytes 2359296 | tf_op jit(solution)/shard_map/all_gather | solution.py:67
  11.2 197.6 %all-gather.14.cloned.1.call-start = ((), (), s32[]{:S(2)}) async-start(), calls=%async_computation.6 | async-start | bytes 2359296 | tf_op jit(solution)/shard_map/all_gather | solution.py:114
  12.0 311.3 %all-gather.20.cloned.1.call-start = ((), (), s32[]{:S(2)}) async-start(), calls=%async_computation.10 | async-start | bytes 4718592 | tf_op jit(solution)/shard_map/all_gather | solution.py:129
  208.8 106.6 %all-to-all-start = ((bf16[4,512,512]{2,1,0:T(8,128)(2,1)}), bf16[4,512,512]{2,1,0:T(8,128)(2,1)}, u32[]{:S(2)}, u32[]{:S(2)}) async-start(bf16[4,512,512]{2,1,0:T(8,128)(2,1)} %bitcast.88), calls=%async_computation | async-start | bytes 4194304 | tf_op jit(solution)/shard_map/all_to_all | solution.py:115
  214.7 166.7 %all-reduce.2.cloned.1.call-start = ((), (), s32[]{:S(2)}) async-start(), calls=%async_computation.7 | async-start | bytes 2097152 | tf_op jit(solution)/shard_map/psum | solution.py:117
  214.9 26.0 %collective-permute-start = (bf16[2,256,4,128]{3,1,2,0:T(8,128)(2,1)S(1)}, bf16[2,256,4,128]{3,1,2,0:T(8,128)(2,1)S(1)}, u32[]{:S(2)}, u32[]{:S(2)}) collective-permute-start(bf16[2,256,4,128]{3,1,2,0:T(8,128)(2,1)S(1)} %get-tuple-element.447), channel_id=1, source_target_pairs={{0,4},{4,8},{8,12},{12,16},{16,20},{20,24},{24,28},{1,5},{5,9},{9,... | collective-permute-start | bytes 1572872 | tf_op jit(solution)/shard_map/while/body/eval_jaxpr/ppermute | solution.py:16
  241.9 19.5 %collective-permute-start = (bf16[2,256,4,128]{3,1,2,0:T(8,128)(2,1)S(1)}, bf16[2,256,4,128]{3,1,2,0:T(8,128)(2,1)S(1)}, u32[]{:S(2)}, u32[]{:S(2)}) collective-permute-start(bf16[2,256,4,128]{3,1,2,0:T(8,128)(2,1)S(1)} %get-tuple-element.447), channel_id=1, source_target_pairs={{0,4},{4,8},{8,12},{12,16},{16,20},{20,24},{24,28},{1,5},{5,9},{9,... | collective-permute-start | bytes 1572872 | tf_op jit(solution)/shard_map/while/body/eval_jaxpr/ppermute | solution.py:16
  262.4 26.4 %collective-permute-start = (bf16[2,256,4,128]{3,1,2,0:T(8,128)(2,1)S(1)}, bf16[2,256,4,128]{3,1,2,0:T(8,128)(2,1)S(1)}, u32[]{:S(2)}, u32[]{:S(2)}) collective-permute-start(bf16[2,256,4,128]{3,1,2,0:T(8,128)(2,1)S(1)} %get-tuple-element.447), channel_id=1, source_target_pairs={{0,4},{4,8},{8,12},{12,16},{16,20},{20,24},{24,28},{1,5},{5,9},{9,... | collective-permute-start | bytes 1572872 | tf_op jit(solution)/shard_map/while/body/eval_jaxpr/ppermute | solution.py:16
  289.9 24.3 %collective-permute-start = (bf16[2,256,4,128]{3,1,2,0:T(8,128)(2,1)S(1)}, bf16[2,256,4,128]{3,1,2,0:T(8,128)(2,1)S(1)}, u32[]{:S(2)}, u32[]{:S(2)}) collective-permute-start(bf16[2,256,4,128]{3,1,2,0:T(8,128)(2,1)S(1)} %get-tuple-element.447), channel_id=1, source_target_pairs={{0,4},{4,8},{8,12},{12,16},{16,20},{20,24},{24,28},{1,5},{5,9},{9,... | collective-permute-start | bytes 1572872 | tf_op jit(solution)/shard_map/while/body/eval_jaxpr/ppermute | solution.py:16
  320.0 2.3 copy-start.2
  320.1 135.3 %all-gather.16.cloned.1.call-start = ((), (), s32[]{:S(2)}) async-start(), calls=%async_computation.8 | async-start | bytes 4718592 | tf_op jit(solution)/shard_map/all_gather | solution.py:124
  322.3 207.1 %all-gather.18.cloned.1.call-start = ((), (), s32[]{:S(2)}) async-start(), calls=%async_computation.9 | async-start | bytes 4718592 | tf_op jit(solution)/shard_map/all_gather | solution.py:125
  323.3 213.3 %all-to-all-start.1 = ((bf16[4,1024,512]{2,1,0:T(8,128)(2,1)}), bf16[4,1024,512]{2,1,0:T(8,128)(2,1)}, u32[]{:S(2)}, u32[]{:S(2)}) async-start(bf16[4,1024,512]{2,1,0:T(8,128)(2,1)} %bitcast.82), calls=%async_computation.1 | async-start | bytes 8388608 | tf_op jit(solution)/shard_map/all_to_all | solution.py:131
  335.5 237.5 %reduce-scatter.2.cloned.1.call-start = ((), (), s32[]{:S(2)}) async-start(), calls=%async_computation.11 | async-start | bytes 1310720 | tf_op jit(solution)/shard_map/reduce_scatter | solution.py:132
Sparse Core Ops, SparseCore 0:
  9.5 49.5 all-gather.9
  61.2 47.7 all-gather.11
  111.2 47.7 all-gather.7
  161.0 47.7 all-gather.13
  210.8 93.5 all-gather.19
  320.2 61.2 all-reduce.1
  383.8 71.5 all-gather.15
  457.7 71.6 all-gather.17
  548.1 24.8 reduce-scatter.1
where the time goes:
time: 583 us; the launch traced here: 581 us
  waiting for transfers between devices  487 us (84%)
  starting transfers between devices  28.4 us (5%)
  matrix products  23 us (4%)
  other arithmetic  17.1 us (3%)
  between operations  13.5 us (2%)
  local copies, waits for them, and re-layouts  11.9 us (2%)
    ppermute x4, waiting for transfers between devices, passed_along(): lax.ppermute(value, axis, [(source, source + steps) for source in range(i...  85 us
    all_gather x1, waiting for transfers between devices, on_device(): lax.all_gather(w_up.astype(half_type), 'dp', axis=0, tiled=True)  74 us
    all_gather x1, waiting for transfers between devices, on_device(): lax.all_gather(w_gate.astype(half_type), 'dp', axis=0, tiled=True)  71.9 us
    all_gather x1, waiting for transfers between devices, on_device(): lax.all_gather(w_query.astype(half_type), 'dp', axis=0, tiled=True)  49.9 us
    all_gather x1, waiting for transfers between devices, on_device(): lax.all_gather(w_value.astype(half_type), 'dp', axis=0, tiled=True)  49.9 us
    psum x1, waiting for transfers between devices, on_device(): lax.psum(partial_out.astype(jnp.bfloat16), 'mp').astype(jnp.float32)  46 us
    all_gather x1, waiting for transfers between devices, on_device(): lax.all_gather(w_key.astype(half_type), 'dp', axis=0, tiled=True)  44.5 us
    all_gather x1, waiting for transfers between devices, on_device(): by_rows = lax.all_gather(w_out.astype(half_type), 'dp', axis=0, tiled=True)  40.7 us
  transfers between devices with their start and end apart: 15, of which 12 were waited for; matrix products, arithmetic and copies ran while one was open for 6% of the time, Pallas kernels for 0%

commit v1 on v0

--- a/solution.py
+++ b/solution.py
@@ -25,7 +25,8 @@
 
 def prompt_coords(first, count, lengths):
     where = first + jnp.arange(count)
-    ends = jnp.cumsum(lengths)
+    upto = jnp.arange(lengths.shape[0])
+    ends = jnp.sum(jnp.where(upto[None, :] <= upto[:, None], lengths[None, :], 0), axis=1)
     passed = (ends[None, :] <= where[:, None]).astype(jnp.int32)
     prompt = jnp.sum(passed, axis=1)
     offset = where - jnp.sum(passed * lengths[None, :], axis=1)
@@ -47,11 +48,6 @@
     )
 
 
-def row_product(left, pieces):
-    block = jnp.concatenate(pieces, axis=1)
-    return jnp.dot(left, block, preferred_element_type=jnp.float32)
-
-
 def on_device(tokens, lengths, w_query, w_key, w_value, w_out, w_gate, w_up, w_down):
     half_type = jnp.bfloat16
     rows = tokens.shape[0]
@@ -61,14 +57,15 @@
     mp_index = lax.axis_index("mp")
     reach = lax.axis_size("dp") // 2
     normed = layer_norm(tokens).astype(half_type)
-    joined = row_product(
-        normed,
-        (
-            lax.all_gather(w_query.astype(half_type), "dp", axis=0, tiled=True),
-            lax.all_gather(w_key.astype(half_type), "dp", axis=0, tiled=True),
-            lax.all_gather(w_value.astype(half_type), "dp", axis=0, tiled=True),
-        ),
-    )
+    packed_in = jnp.concatenate([w.astype(half_type) for w in (w_query, w_key, w_value)], axis=1)
+    server_in = lax.all_gather(packed_in, "dp", axis=0, tiled=True)
+    packed_mid = jnp.concatenate([w.astype(half_type) for w in (w_out, w_gate, w_up)], axis=1)
+    down = w_down.astype(half_type)
+    server_in, packed_mid, down = lax.optimization_barrier((server_in, packed_mid, down))
+    server_mid = lax.all_gather(packed_mid, "dp", axis=0, tiled=True)
+    server_mid, down = lax.optimization_barrier((server_mid, down))
+    server_down = lax.all_gather(down, "dp", axis=0, tiled=True)
+    joined = jnp.dot(normed, server_in, preferred_element_type=jnp.float32)
     q_prompt, q_offset, q_where = prompt_coords(dp_index * rows, rows, lengths)
     shaped = joined.reshape(rows, 3, heads_dev, HEAD)
     query = rotate(shaped[:, 0], q_offset).astype(half_type)
@@ -111,32 +108,19 @@
     unused, state = lax.fori_loop(0, reach, relay_step, (own_pair, state))
     accum, total, top = state
     context = (accum / jnp.transpose(total, (1, 0, 2))).astype(half_type).reshape(rows, narrow)
-    by_rows = lax.all_gather(w_out.astype(half_type), "dp", axis=0, tiled=True)
-    server_out = lax.all_to_all(by_rows, "mp", split_axis=0, concat_axis=1, tiled=True)
-    partial_out = jnp.dot(context, server_out, preferred_element_type=jnp.float32)
-    attended = lax.psum(partial_out.astype(jnp.bfloat16), "mp").astype(jnp.float32)
-    mixed = (tokens.astype(jnp.float32) + attended).astype(half_type)
+    all_heads = lax.all_gather(context, "mp", axis=1, tiled=True)
+    attended = jnp.dot(all_heads, server_mid[:, :narrow], preferred_element_type=jnp.float32)
+    own_columns = lax.dynamic_slice_in_dim(tokens, mp_index * narrow, narrow, 1)
+    own_mixed = (own_columns.astype(jnp.float32) + attended).astype(half_type)
+    mixed = lax.all_gather(own_mixed, "mp", axis=1, tiled=True)
     normed_two = layer_norm(mixed).astype(half_type)
     units = w_gate.shape[1]
-    gate_up = row_product(
-        normed_two,
-        (
-            lax.all_gather(w_gate.astype(half_type), "dp", axis=0, tiled=True),
-            lax.all_gather(w_up.astype(half_type), "dp", axis=0, tiled=True),
-        ),
-    )
+    gate_up = jnp.dot(normed_two, server_mid[:, narrow:], preferred_element_type=jnp.float32)
     hidden = (jax.nn.silu(gate_up[:, :units]) * gate_up[:, units:]).astype(half_type)
-    gathered_down = lax.all_gather(w_down.astype(half_type), "dp", axis=0, tiled=True)
-    slab = rows // lax.axis_size("mp")
-    server_down = lax.all_to_all(gathered_down, "mp", split_axis=0, concat_axis=1, tiled=True)
-    share = lax.psum_scatter(
-        jnp.dot(hidden, server_down, preferred_element_type=jnp.float32).astype(jnp.bfloat16),
-        "mp",
-        scatter_dimension=0,
-        tiled=True,
-    ).astype(jnp.float32)
-    own_rows = lax.dynamic_slice_in_dim(mixed, mp_index * slab, slab, 0)
-    return (own_rows.astype(jnp.float32) + share).astype(half_type)
+    all_hidden = lax.all_gather(hidden, "mp", axis=1, tiled=True)
+    product = jnp.dot(all_hidden, server_down, preferred_element_type=jnp.float32)
+    own_out = (own_mixed.astype(jnp.float32) + product).astype(half_type)
+    return lax.all_to_all(own_out, "mp", split_axis=0, concat_axis=1, tiled=True)
 
 
 def solution(mesh):

time: 583 us -> 473 us (0.81)
  waiting for transfers between devices: 487 us -> 367 us
  blocking collectives: 0 us -> 9.24 us
  local copies, waits for them, and re-layouts: 11.9 us -> 3.89 us
  starting transfers between devices: 28.4 us -> 35.1 us
    psum x1 -> x0, waiting for transfers between devices: 46 us -> none  [on_device(): lax.psum(partial_out.astype(jnp.bfloat16), 'mp').astype(jnp.float32)]
    all_gather x7 -> x6, waiting for transfers between devices: 331 us -> 298 us  [the longest x1 94.3 us: on_device(): server_in = lax.all_gather(packed_in, 'dp', axis=0, tiled=True)]
    reduce_scatter x1 -> x0, waiting for transfers between devices: 25 us -> none  [on_device(): lax.psum_scatter(jnp.dot(hidden, server_down, preferred_element_type=jnp....]
    ppermute x4, starting transfers between devices: 10 us -> 34.9 us  [passed_along(): lax.ppermute(value, axis, [(source, source + steps) for source in range(i...]
    all_to_all x2 -> x0, starting transfers between devices: 18.1 us -> none  [the longest x1 12.2 us: on_device(): lax.all_to_all(gathered_down, 'mp', split_axis=0, concat_axis=1, tiled=True)]
    ppermute x4, waiting for transfers between devices: 85 us -> 69.1 us  [passed_along(): lax.ppermute(value, axis, [(source, source + steps) for source in range(i...]
    all_to_all x0 -> x1, blocking collectives: none -> 9.24 us  [on_device(): lax.all_to_all(own_out, 'mp', split_axis=0, concat_axis=1, tiled=True)]
    all_to_all x2 -> x1, local copies, waits for them, and re-layouts: 9.09 us -> 0.73 us  [on_device(): lax.all_to_all(own_out, 'mp', split_axis=0, concat_axis=1, tiled=True)]
  transfers between devices with their start and end apart: 15 -> 10, of which waited for: 12 -> 10; matrix products, arithmetic and copies ran while one was open for 6% -> 4% of each run, Pallas kernels for 0% -> 0%
where the time goes in v1:
time: 473 us; the launch traced here: 470 us
  waiting for transfers between devices  367 us (78%)
  starting transfers between devices  35.1 us (7%)
  matrix products  22.8 us (5%)
  other arithmetic  17.2 us (4%)
  between operations  13.8 us (3%)
  blocking collectives  9.24 us (2%)
    all_gather x1, waiting for transfers between devices, on_device(): server_in = lax.all_gather(packed_in, 'dp', axis=0, tiled=True)  94.3 us
    all_gather x1, waiting for transfers between devices, on_device(): server_down = lax.all_gather(down, 'dp', axis=0, tiled=True)  73.3 us
    all_gather x1, waiting for transfers between devices, on_device(): server_mid = lax.all_gather(packed_mid, 'dp', axis=0, tiled=True)  70.6 us
    ppermute x4, waiting for transfers between devices, passed_along(): lax.ppermute(value, axis, [(source, source + steps) for source in range(i...  69.1 us
    ppermute x4, starting transfers between devices, passed_along(): lax.ppermute(value, axis, [(source, source + steps) for source in range(i...  34.9 us
    all_gather x1, waiting for transfers between devices, on_device(): all_hidden = lax.all_gather(hidden, 'mp', axis=1, tiled=True)  22.2 us
    all_gather x1, waiting for transfers between devices, on_device(): all_heads = lax.all_gather(context, 'mp', axis=1, tiled=True)  20.5 us
    all_gather x1, waiting for transfers between devices, on_device(): mixed = lax.all_gather(own_mixed, 'mp', axis=1, tiled=True)  16.8 us
  transfers between devices with their start and end apart: 10, of which 10 were waited for; matrix products, arithmetic and copies ran while one was open for 4% of the time, Pallas kernels for 0%

profile of v1, /device:TPU:9, one launch (start us, length us, event | category | flops | bytes accessed | tf_op | source)
XLA Modules:
  0.0 469.8 jit_solution(2007033715421453534)
XLA Ops:
  6.5 1.1 convert_element_type.108
  7.6 1.2 convert_element_type.109
  8.8 1.1 convert_element_type.110
  9.9 0.9 pad_maximum_fusion.1
  11.0 0.4 copy-done.3
  11.5 1.1 convert_element_type.111
  12.6 0.9 convert_element_type.114
  13.4 1.2 pad_maximum_fusion
  14.6 94.3 %all-gather.7.cloned.1.call-done = bf16[2048,1536]{1,0:T(8,128)(2,1)} async-done(((bf16[256,1536]{1,0:T(8,128)(2,1)}), bf16[2048,1536]{1,0:T(8,128)(2,1)}) %all-gather.7.cloned.1.call-update) | async-done | bytes 6291472 | tf_op jit(solution)/shard_map/all_gather | solution.py:61
  109.5 0.4 fusion.17
  110.0 0.5 multiply_cosine_fusion
  110.6 5.8 %fusion.30 = f32[256,1536]{1,0:T(8,128)} fusion(bf16[2048,1536]{1,0:T(8,128)(2,1)} %all-gather.7.cloned.1.call-done, bf16[256,2048]{1,0:T(8,128)(2,1)S(1)} %copy-done, f32[256]{0:T(256)S(1)} %add_rsqrt_fusion.1, f32[256]{0:T(256)S(1)} %broadcast_multiply_fusion.1), kind=kOutput, calls=%fused_computation.47 | convolution fusion | flops 1612709888 | bytes 8914944 | tf_op jit(solution)/shard_map/dot_general | solution.py:68
  116.4 1.8 reshape.318
  118.6 0.4 subtract_convert_fusion
  119.2 0.4 fusion.53
  119.8 0.3 fusion.25
  120.5 109.7 %while.21 = (s32[]{:T(128)}, bf16[2,256,4,128]{3,1,2,0:T(8,128)(2,1)S(1)}, f32[256,4,128]{2,0,1:T(8,128)S(1)}, f32[4,256,1]{1,0,2:T(4,128)S(1)}, f32[4,256,1]{1,...) while((s32[]{:T(128)}, ...), condition=%wide.region_12.13_spmd.clone.clone, body=%wide.region_7.12_spmd.clone.clone.sunk | while | flops 136518704 | bytes 8333545 | solution.py:108
  120.5 2.4 collective-permute-start
  123.3 24.6 %collective-permute-done = bf16[2,256,4,128]{3,1,2,0:T(8,128)(2,1)S(1)} collective-permute-done((bf16[2,256,4,128]{3,1,2,0:T(8,128)(2,1)S(1)}, bf16[2,256,4,128]{3,1,2,0:T(8,128)(2,1)S(1)}, u32[]{:S(2)}, u32[]{:S(2)}) %collective-permute-start) | collective-permute-done | bytes 524320 | tf_op jit(solution)/shard_map/while/body/eval_jaxpr/ppermute | solution.py:16
  147.9 0.3 fusion.68
  148.4 0.5 fusion.70
  148.9 10.8 %collective-permute-start = (bf16[2,256,4,128]{3,1,2,0:T(8,128)(2,1)S(1)}, bf16[2,256,4,128]{3,1,2,0:T(8,128)(2,1)S(1)}, u32[]{:S(2)}, u32[]{:S(2)}) collective-permute-start(bf16[2,256,4,128]{3,1,2,0:T(8,128)(2,1)S(1)} %get-tuple-element.382), channel_id=1, source_target_pairs={{0,4},{4,8},{8,12},{12,16},{16,20},{20,24},{24,28},{1,5},{5,9},{9,... | collective-permute-start | bytes 1572872 | tf_op jit(solution)/shard_map/while/body/eval_jaxpr/ppermute | solution.py:16
  160.1 15.8 %collective-permute-done = bf16[2,256,4,128]{3,1,2,0:T(8,128)(2,1)S(1)} collective-permute-done((bf16[2,256,4,128]{3,1,2,0:T(8,128)(2,1)S(1)}, bf16[2,256,4,128]{3,1,2,0:T(8,128)(2,1)S(1)}, u32[]{:S(2)}, u32[]{:S(2)}) %collective-permute-start) | collective-permute-done | bytes 524320 | tf_op jit(solution)/shard_map/while/body/eval_jaxpr/ppermute | solution.py:16
  175.9 0.3 fusion.68
  176.5 0.5 fusion.70
  177.0 11.2 %collective-permute-start = (bf16[2,256,4,128]{3,1,2,0:T(8,128)(2,1)S(1)}, bf16[2,256,4,128]{3,1,2,0:T(8,128)(2,1)S(1)}, u32[]{:S(2)}, u32[]{:S(2)}) collective-permute-start(bf16[2,256,4,128]{3,1,2,0:T(8,128)(2,1)S(1)} %get-tuple-element.382), channel_id=1, source_target_pairs={{0,4},{4,8},{8,12},{12,16},{16,20},{20,24},{24,28},{1,5},{5,9},{9,... | collective-permute-start | bytes 1572872 | tf_op jit(solution)/shard_map/while/body/eval_jaxpr/ppermute | solution.py:16
  188.6 9.9 %collective-permute-done = bf16[2,256,4,128]{3,1,2,0:T(8,128)(2,1)S(1)} collective-permute-done((bf16[2,256,4,128]{3,1,2,0:T(8,128)(2,1)S(1)}, bf16[2,256,4,128]{3,1,2,0:T(8,128)(2,1)S(1)}, u32[]{:S(2)}, u32[]{:S(2)}) %collective-permute-start) | collective-permute-done | bytes 524320 | tf_op jit(solution)/shard_map/while/body/eval_jaxpr/ppermute | solution.py:16
  198.4 0.3 fusion.68
  199.0 0.5 fusion.70
  199.5 10.4 %collective-permute-start = (bf16[2,256,4,128]{3,1,2,0:T(8,128)(2,1)S(1)}, bf16[2,256,4,128]{3,1,2,0:T(8,128)(2,1)S(1)}, u32[]{:S(2)}, u32[]{:S(2)}) collective-permute-start(bf16[2,256,4,128]{3,1,2,0:T(8,128)(2,1)S(1)} %get-tuple-element.382), channel_id=1, source_target_pairs={{0,4},{4,8},{8,12},{12,16},{16,20},{20,24},{24,28},{1,5},{5,9},{9,... | collective-permute-start | bytes 1572872 | tf_op jit(solution)/shard_map/while/body/eval_jaxpr/ppermute | solution.py:16
  210.3 18.8 %collective-permute-done = bf16[2,256,4,128]{3,1,2,0:T(8,128)(2,1)S(1)} collective-permute-done((bf16[2,256,4,128]{3,1,2,0:T(8,128)(2,1)S(1)}, bf16[2,256,4,128]{3,1,2,0:T(8,128)(2,1)S(1)}, u32[]{:S(2)}, u32[]{:S(2)}) %collective-permute-start) | collective-permute-done | bytes 524320 | tf_op jit(solution)/shard_map/while/body/eval_jaxpr/ppermute | solution.py:16
  229.1 0.3 fusion.68
  229.7 0.5 fusion.70
  230.4 0.7 divide_convert_fusion
  231.2 70.6 %all-gather.11.cloned.1.call-done = bf16[2048,2560]{1,0:T(8,128)(2,1)} async-done(((bf16[256,2560]{1,0:T(8,128)(2,1)}), bf16[2048,2560]{1,0:T(8,128)(2,1)}) %all-gather.11.cloned.1.call-update) | async-done | bytes 10485776 | tf_op jit(solution)/shard_map/all_gather | solution.py:65
  301.9 20.5 %all-gather.9.cloned.1.call-done = bf16[256,2048]{0,1:T(8,128)(2,1)} async-done(((bf16[256,512]{0,1:T(8,128)(2,1)}), bf16[256,2048]{0,1:T(8,128)(2,1)}) %all-gather.9.cloned.1.call-update) | async-done | bytes 1048592 | tf_op jit(solution)/shard_map/all_gather | solution.py:111
  322.4 3.3 fusion.26
  325.8 16.8 %all-gather.13.cloned.1.call-done = bf16[256,2048]{1,0:T(8,128)(2,1)} async-done(((bf16[256,512]{1,0:T(8,128)(2,1)}), bf16[256,2048]{1,0:T(8,128)(2,1)}) %all-gather.13.cloned.1.call-update) | async-done | bytes 1048592 | tf_op jit(solution)/shard_map/all_gather | solution.py:115
  342.6 1.5 convert_reduce_fusion.1
  344.2 1.6 fusion.15
  345.8 5.8 %fusion.9 = f32[256,2048]{1,0:T(8,128)S(1)} fusion(bf16[2048,2560]{1,0:T(8,128)(2,1)} %all-gather.11.cloned.1.call-done, bf16[256,2048]{1,0:T(8,128)(2,1)S(1)} %copy-done.1, f32[256]{0:T(256)S(1)} %add_rsqrt_fusion, f32[256]{0:T(256)S(1)} %broadcast_multiply_fusion), kind=kOutput, calls=%fused_computation.22 | convolution fusion | flops 2149580800 | bytes 11536384 | tf_op jit(solution)/shard_map/dot_general | solution.py:118
  351.6 1.1 fusion.33
  352.8 0.5 all-gather.17.cloned.1.call-update
  353.4 22.2 %all-gather.15.cloned.1.call-done = bf16[256,4096]{1,0:T(8,128)(2,1)} async-done(((bf16[256,1024]{1,0:T(8,128)(2,1)}), bf16[256,4096]{1,0:T(8,128)(2,1)}) %all-gather.15.cloned.1.call-update) | async-done | bytes 2097168 | tf_op jit(solution)/shard_map/all_gather | solution.py:120
  375.5 73.3 %all-gather.17.cloned.1.call-done = bf16[4096,512]{1,0:T(8,128)(2,1)} async-done(((bf16[512,512]{1,0:T(8,128)(2,1)}), bf16[4096,512]{1,0:T(8,128)(2,1)}) %all-gather.17.cloned.1.call-update) | async-done | bytes 4194320 | tf_op jit(solution)/shard_map/all_gather | solution.py:67
  448.9 4.1 fusion.29
  452.9 9.2 %all_to_all.19 = bf16[4,64,512]{2,1,0:T(8,128)(2,1)S(1)} all-to-all(bf16[4,64,512]{2,1,0:T(8,128)(2,1)S(1)} %bitcast.83), channel_id=1, replica_groups=mesh['dp'=8,'mp'=4] {'mp'}, dimensions={0} | all-to-all | bytes 524288 | tf_op jit(solution)/shard_map/all_to_all | solution.py:123
  462.2 0.7 copy.42
  (87 shorter events, 4.6 us)
Async XLA Ops:
  6.5 102.4 %all-gather.7.cloned.1.call-start = ((), (), s32[]{:S(2)}) async-start(), calls=%async_computation.1 | async-start | bytes 7077888 | tf_op jit(solution)/shard_map/all_gather | solution.py:61
  7.6 3.3 copy-start.2
  9.9 1.5 copy-start.3
  10.8 291.0 %all-gather.11.cloned.1.call-start = ((), (), s32[]{:S(2)}) async-start(), calls=%async_computation.3 | async-start | bytes 11796480 | tf_op jit(solution)/shard_map/all_gather | solution.py:65
  10.9 1.6 copy-start.4
  13.4 95.6 %copy-start.6 = (s32[4]{0:T(128)S(1)}, s32[4]{0:T(128)}, u32[]{:S(2)}) copy-start(s32[4]{0:T(128)} %param.12) | copy-start | bytes 52
  13.4 95.8 %copy-start = (bf16[256,2048]{1,0:T(8,128)(2,1)S(1)}, bf16[256,2048]{1,0:T(8,128)(2,1)}, u32[]{:S(2)}) copy-start(bf16[256,2048]{1,0:T(8,128)(2,1)} %param.11) | copy-start | bytes 3145732
  108.9 213.4 %all-gather.9.cloned.1.call-start = ((), (), s32[]{:S(2)}) async-start(), calls=%async_computation.2 | async-start | bytes 1310720 | tf_op jit(solution)/shard_map/all_gather | solution.py:111
  120.5 27.4 %collective-permute-start = (bf16[2,256,4,128]{3,1,2,0:T(8,128)(2,1)S(1)}, bf16[2,256,4,128]{3,1,2,0:T(8,128)(2,1)S(1)}, u32[]{:S(2)}, u32[]{:S(2)}) collective-permute-start(bf16[2,256,4,128]{3,1,2,0:T(8,128)(2,1)S(1)} %get-tuple-element.382), channel_id=1, source_target_pairs={{0,4},{4,8},{8,12},{12,16},{16,20},{20,24},{24,28},{1,5},{5,9},{9,... | collective-permute-start | bytes 1572872 | tf_op jit(solution)/shard_map/while/body/eval_jaxpr/ppermute | solution.py:16
  148.9 27.0 %collective-permute-start = (bf16[2,256,4,128]{3,1,2,0:T(8,128)(2,1)S(1)}, bf16[2,256,4,128]{3,1,2,0:T(8,128)(2,1)S(1)}, u32[]{:S(2)}, u32[]{:S(2)}) collective-permute-start(bf16[2,256,4,128]{3,1,2,0:T(8,128)(2,1)S(1)} %get-tuple-element.382), channel_id=1, source_target_pairs={{0,4},{4,8},{8,12},{12,16},{16,20},{20,24},{24,28},{1,5},{5,9},{9,... | collective-permute-start | bytes 1572872 | tf_op jit(solution)/shard_map/while/body/eval_jaxpr/ppermute | solution.py:16
  177.0 21.4 %collective-permute-start = (bf16[2,256,4,128]{3,1,2,0:T(8,128)(2,1)S(1)}, bf16[2,256,4,128]{3,1,2,0:T(8,128)(2,1)S(1)}, u32[]{:S(2)}, u32[]{:S(2)}) collective-permute-start(bf16[2,256,4,128]{3,1,2,0:T(8,128)(2,1)S(1)} %get-tuple-element.382), channel_id=1, source_target_pairs={{0,4},{4,8},{8,12},{12,16},{16,20},{20,24},{24,28},{1,5},{5,9},{9,... | collective-permute-start | bytes 1572872 | tf_op jit(solution)/shard_map/while/body/eval_jaxpr/ppermute | solution.py:16
  199.5 29.7 %collective-permute-start = (bf16[2,256,4,128]{3,1,2,0:T(8,128)(2,1)S(1)}, bf16[2,256,4,128]{3,1,2,0:T(8,128)(2,1)S(1)}, u32[]{:S(2)}, u32[]{:S(2)}) collective-permute-start(bf16[2,256,4,128]{3,1,2,0:T(8,128)(2,1)S(1)} %get-tuple-element.382), channel_id=1, source_target_pairs={{0,4},{4,8},{8,12},{12,16},{16,20},{20,24},{24,28},{1,5},{5,9},{9,... | collective-permute-start | bytes 1572872 | tf_op jit(solution)/shard_map/while/body/eval_jaxpr/ppermute | solution.py:16
  231.2 111.5 %all-gather.13.cloned.1.call-start = ((), (), s32[]{:S(2)}) async-start(), calls=%async_computation.4 | async-start | bytes 1310720 | tf_op jit(solution)/shard_map/all_gather | solution.py:115
  325.7 49.8 %all-gather.15.cloned.1.call-start = ((), (), s32[]{:S(2)}) async-start(), calls=%async_computation.5 | async-start | bytes 2621440 | tf_op jit(solution)/shard_map/all_gather | solution.py:120
  342.6 3.2 copy-start.1
  351.6 97.3 %copy-start.5 = (bf16[256,512]{1,0:T(8,128)(2,1)S(1)}, bf16[256,512]{1,0:T(8,128)(2,1)}, u32[]{:S(2)}) copy-start(bf16[256,512]{1,0:T(8,128)(2,1)} %fusion.26) | copy-start | bytes 786436
  352.8 96.1 %all-gather.17.cloned.1.call-start = ((), (), s32[]{:S(2)}) async-start(), calls=%async_computation.6 | async-start | bytes 4718592 | tf_op jit(solution)/shard_map/all_gather | solution.py:67
Sparse Core Ops, SparseCore 0:
  11.0 97.8 all-gather.6
  111.1 190.7 all-gather.10
  303.4 18.8 all-gather.8
  325.9 16.7 all-gather.12
  352.9 22.5 all-gather.14
  377.5 71.3 all-gather.16

commit v2 on v1

--- a/solution.py
+++ b/solution.py
@@ -1,6 +1,10 @@
+import functools
+
 import jax
 import jax.numpy as jnp
 from jax import lax
+from jax.experimental import pallas as pl
+from jax.experimental.pallas import tpu as pltpu
 from jax.sharding import PartitionSpec as P
 
 HEAD = 128
@@ -123,6 +127,339 @@
     return lax.all_to_all(own_out, "mp", split_axis=0, concat_axis=1, tiled=True)
 
 
+def place():
+    dp_index, mp_index = lax.axis_index("dp"), lax.axis_index("mp")
+    return dp_index // 2, dp_index % 2, mp_index // 2, mp_index % 2
+
+
+def device(z, y, x, c):
+    return (2 * z + y, 2 * x + c)
+
+
+def remote(source, target, send, receive, where):
+    return pltpu.make_async_remote_copy(
+        src_ref=source,
+        dst_ref=target,
+        send_sem=send,
+        recv_sem=receive,
+        device_id=where,
+        device_id_type=pl.DeviceIdType.MESH,
+    )
+
+
+def greet(peers):
+    barrier = pltpu.get_barrier_semaphore()
+    for peer in peers:
+        pl.semaphore_signal(barrier, inc=1, device_id=peer, device_id_type=pl.DeviceIdType.MESH)
+    pl.semaphore_wait(barrier, len(peers))
+
+
+def plane_peers(z, y, x, c):
+    return [device(z, y, 1 - x, c), device(z, 1 - y, x, c), device(z, 1 - y, 1 - x, c)]
+
+
+def column_peers(z, y, x, c):
+    steps = [(k, f) for k in range(4) for f in range(2) if k or f]
+    return [(k, f, device((z + k) % 4, y, x, (c + f) % 2)) for k, f in steps]
+
+
+def regroup_kernel(
+    in_ref, mid_ref, out_ref, down_ref, rows_ref,
+    in_all, mid_all, out_all, down_all, rows_all,
+    column_send, column_recv, plane_send, plane_recv,
+    part_send, part_recv, fan_send, fan_recv, local_sem,
+):
+    z, y, x, c = place()
+    own = 2 * z + y
+    plane = plane_peers(z, y, x, c)
+    greet([peer for _, _, peer in column_peers(z, y, x, c)] + plane)
+    width = out_ref.shape[-1]
+
+    def columns(mp):
+        return pl.ds(pl.multiple_of(mp * width, width), width)
+
+    packs = ((in_ref, in_all), (mid_ref, mid_all))
+    locals_ = []
+    for i, (source, target) in enumerate(packs):
+        locals_.append(pltpu.make_async_copy(source.at[z], target.at[x, own], local_sem.at[i]))
+    locals_.append(pltpu.make_async_copy(rows_ref, rows_all.at[z], local_sem.at[2]))
+    for copy in locals_:
+        copy.start()
+    sends = []
+
+    def column_copy(i, k):
+        to = (z + k) % 4
+        source, target = packs[i] if i < 2 else (rows_ref, rows_all)
+        source = source.at[to] if i < 2 else source
+        target = target.at[x, own] if i < 2 else target.at[z]
+        return remote(source, target, column_send.at[i, k], column_recv.at[i, k], device(to, y, x, c))
+
+    halves = ((out_ref, out_all), (down_ref, down_all))
+    hub = y == z // 2
+
+    def part_copy(i, hf):
+        source, target = halves[i]
+        slot = (z // 2) * 2 + c
+        return (
+            source.at[hf],
+            target.at[z // 2, :, columns(2 * x + c)],
+            part_send.at[i, hf],
+            part_recv.at[i, slot],
+        )
+
+    def is_self(hf):
+        return (2 * y + hf == z) & (z % 2 == c)
+
+    for k in (1, 3, 2):
+        copy = column_copy(0, k)
+        copy.start()
+        sends.append(copy)
+    for k in (1, 3, 2):
+        copy = column_copy(2, k)
+        copy.start()
+        sends.append(copy)
+    for i in range(2):
+        for hf in range(2):
+            source, target, send, receive = part_copy(i, hf)
+
+            @pl.when(is_self(hf))
+            def _():
+                pltpu.make_async_copy(source, target, receive).start()
+
+            @pl.when(jnp.logical_not(is_self(hf)))
+            def _():
+                remote(source, target, send, receive, device(2 * y + hf, y, x, z % 2)).start()
+    for k in (1, 3, 2):
+        copy = column_copy(1, k)
+        copy.start()
+        sends.append(copy)
+
+    def fan_copies(i, k):
+        block = packs[i][1].at[x, 2 * ((z + 4 - k) % 4) + y]
+        return [
+            remote(block, block, plane_send.at[i, k, f], plane_recv.at[i, k, f], peer)
+            for f, peer in enumerate(plane)
+        ]
+
+    def part_block(i, p):
+        return halves[i][1].at[p // 2, :, columns(2 * x + p % 2)]
+
+    def part_fan(i, p):
+        block = part_block(i, p)
+        return [
+            remote(block, block, fan_send.at[i, p, f], fan_recv.at[i, p, f], peer)
+            for f, peer in enumerate(plane)
+        ]
+
+    def forward(i):
+        for k in (0, 1, 3, 2):
+            if k == 0:
+                locals_[i].wait()
+            else:
+                column_copy(i, k).wait_recv()
+            for copy in fan_copies(i, k):
+                copy.start()
+
+    forward(0)
+
+    @pl.when(hub)
+    def _():
+        for i in range(2):
+            for p in range(4):
+                block = part_block(i, p)
+                pltpu.make_async_copy(block, block, part_recv.at[i, p]).wait()
+                for copy in part_fan(i, p):
+                    copy.start()
+
+    forward(1)
+    locals_[2].wait()
+    for k in (1, 3, 2):
+        column_copy(2, k).wait_recv()
+    for copy in sends:
+        copy.wait_send()
+    for i in range(2):
+        for hf in range(2):
+            source, target, send, receive = part_copy(i, hf)
+
+            @pl.when(jnp.logical_not(is_self(hf)))
+            def _():
+                remote(source, target, send, receive, device(2 * y + hf, y, x, z % 2)).wait_send()
+        for k in range(4):
+            for copy in fan_copies(i, k):
+                copy.wait()
+
+    @pl.when(hub)
+    def _():
+        for i in range(2):
+            for p in range(4):
+                for copy in part_fan(i, p):
+                    copy.wait_send()
+                part_fan(i, p)[0].wait_recv()
+
+    @pl.when(jnp.logical_not(hub))
+    def _():
+        for i in range(2):
+            for p in range(4):
+                for copy in part_fan(i, p)[1:]:
+                    copy.wait_recv()
+
+
+def any_spec():
+    return pl.BlockSpec(memory_space=pl.ANY)
+
+
+def regroup(*arrays):
+    packed_in, packed_mid, out, down, rows = arrays
+    half_type = jnp.bfloat16
+    depth, cols_in = packed_in.shape[1:]
+    cols_mid = packed_mid.shape[2]
+    shapes = (
+        (2, 8, depth, cols_in),
+        (2, 8, depth, cols_mid),
+        (2, out.shape[1], 4 * out.shape[2]),
+        (2, down.shape[1], 4 * down.shape[2]),
+        (4, *rows.shape),
+    )
+    dma = pltpu.SemaphoreType.DMA
+    return pl.pallas_call(
+        regroup_kernel,
+        out_shape=[jax.ShapeDtypeStruct(shape, half_type) for shape in shapes],
+        in_specs=[any_spec()] * 5,
+        out_specs=[any_spec()] * 5,
+        scratch_shapes=[
+            dma((3, 4)), dma((3, 4)), dma((2, 4, 3)), dma((2, 4, 3)),
+            dma((2, 2)), dma((2, 4)), dma((2, 4, 3)), dma((2, 4, 3)), dma((3,)),
+        ],
+        compiler_params=pltpu.CompilerParams(collective_id=0, has_side_effects=True, vmem_limit_bytes=1 << 20),
+    )(*arrays)
+
+
+def plane_kernel(block_ref, all_ref, send, receive, local_sem):
+    z, y, x, c = place()
+    peers = plane_peers(z, y, x, c)
+    greet(peers)
+    target = all_ref.at[2 * x + y]
+    copies = [remote(block_ref, target, send.at[f], receive.at[f], p) for f, p in enumerate(peers)]
+    own = pltpu.make_async_copy(block_ref, target, local_sem)
+    for copy in copies:
+        copy.start()
+    own.start()
+    own.wait()
+    for copy in copies:
+        copy.wait()
+
+
+def plane_gather(block):
+    dma = pltpu.SemaphoreType.DMA
+    return pl.pallas_call(
+        plane_kernel,
+        out_shape=jax.ShapeDtypeStruct((4, *block.shape), block.dtype),
+        in_specs=[any_spec()],
+        out_specs=any_spec(),
+        scratch_shapes=[dma((3,)), dma((3,)), dma(())],
+        compiler_params=pltpu.CompilerParams(collective_id=1, has_side_effects=True, vmem_limit_bytes=1 << 20),
+    )(block)
+
+
+def column_kernel(split, block_ref, all_ref, send, receive, local_sem):
+    z, y, x, c = place()
+    peers = column_peers(z, y, x, c)
+    greet([peer for _, _, peer in peers])
+    target = all_ref.at[2 * z + c]
+    copies = []
+    for k, f, peer in peers:
+        source = block_ref.at[2 * ((z + k) % 4) + (c + f) % 2] if split else block_ref
+        copies.append(remote(source, target, send.at[k, f], receive.at[k, f], peer))
+    for copy in copies:
+        copy.start()
+    own = pltpu.make_async_copy(block_ref.at[2 * z + c] if split else block_ref, target, local_sem)
+    own.start()
+    own.wait()
+    for copy in copies:
+        copy.wait()
+
+
+def column_exchange(block, split, number):
+    dma = pltpu.SemaphoreType.DMA
+    shape = block.shape if split else (8, *block.shape)
+    return pl.pallas_call(
+        functools.partial(column_kernel, split),
+        out_shape=jax.ShapeDtypeStruct(shape, block.dtype),
+        in_specs=[any_spec()],
+        out_specs=any_spec(),
+        scratch_shapes=[dma((4, 2)), dma((4, 2)), dma(())],
+        compiler_params=pltpu.CompilerParams(collective_id=number, has_side_effects=True, vmem_limit_bytes=1 << 20),
+    )(block)
+
+
+def prompt_at(where, lengths):
+    upto = jnp.arange(lengths.shape[0])
+    ends = jnp.sum(jnp.where(upto[None, :] <= upto[:, None], lengths[None, :], 0), axis=1)
+    passed = (ends[None, :] <= where[:, None]).astype(jnp.int32)
+    return jnp.sum(passed, axis=1), where - jnp.sum(passed * lengths[None, :], axis=1)
+
+
+def regrouped(tokens, lengths, w_query, w_key, w_value, w_out, w_gate, w_up, w_down):
+    half_type = jnp.bfloat16
+    z, y, x, c = place()
+    rows, width = tokens.shape
+    depth, narrow = w_query.shape
+    units = w_gate.shape[1] // 4
+    slab = rows // 4
+
+    def pieces(weight):
+        return weight.astype(half_type).reshape(weight.shape[0], 4, -1)
+
+    packed_in = jnp.concatenate([pieces(w) for w in (w_query, w_key, w_value)], axis=2).transpose(1, 0, 2)
+    packed_mid = jnp.concatenate([pieces(w) for w in (w_gate, w_up)], axis=2).transpose(1, 0, 2)
+    out = w_out.astype(half_type).reshape(2, -1, narrow)
+    down = w_down.astype(half_type).reshape(2, -1, narrow)
+    chip_rows = lax.dynamic_slice_in_dim(tokens, x * 2 * slab, 2 * slab, 0)
+    normed = layer_norm(chip_rows).astype(half_type)
+    server_in, server_mid, server_out, server_down, normed = regroup(packed_in, packed_mid, out, down, normed)
+    count = 8 * slab
+    normed = normed.reshape(count, width)
+    server_in = server_in.reshape(2, width, 3 * HEAD)
+    server_mid = server_mid.reshape(2, width, 2 * units)
+    where = (
+        jnp.arange(4)[:, None] * (2 * rows) + jnp.arange(2 * slab)[None, :]
+    ).reshape(-1)
+    q_where = where + y * rows + x * (2 * slab)
+    q_prompt, q_offset = prompt_at(q_where, lengths)
+    corner = jnp.arange(4)
+    k_where = (((corner % 2) * rows + (corner // 2) * (2 * slab))[:, None] + where[None, :]).reshape(-1)
+    k_prompt, _ = prompt_at(k_where, lengths)
+    joined = [jnp.dot(normed, server_in[i], preferred_element_type=jnp.float32) for i in range(2)]
+    query = rotate(jnp.stack([j[:, :HEAD] for j in joined], axis=1), q_offset).astype(half_type)
+    keys = rotate(jnp.stack([j[:, HEAD : 2 * HEAD] for j in joined], axis=1), q_offset).astype(half_type)
+    block = jnp.concatenate(
+        [keys.reshape(count, -1)] + [j[:, 2 * HEAD :].astype(half_type) for j in joined], axis=1
+    )
+    pairs = plane_gather(block).reshape(4 * count, 4, HEAD)
+    allowed = (q_prompt[:, None] == k_prompt[None, :]) & (k_where[None, :] <= q_where[:, None])
+    scale = 1.0 / HEAD**0.5
+    scores = jnp.einsum("qhd,khd->hqk", query, pairs[:, :2], preferred_element_type=jnp.float32) * scale
+    scores = jnp.where(allowed[None], scores, -jnp.inf)
+    weights = jnp.exp(scores - jnp.max(scores, axis=-1, keepdims=True))
+    total = jnp.sum(weights, axis=-1)
+    accum = jnp.einsum("hqk,khd->qhd", weights.astype(half_type), pairs[:, 2:], preferred_element_type=jnp.float32)
+    context = (accum / total.T[:, :, None]).astype(half_type).reshape(count, 2 * HEAD)
+    partial = jnp.dot(context, server_out.reshape(2 * HEAD, width), preferred_element_type=jnp.float32)
+    shares = column_exchange(partial.astype(half_type).reshape(8, slab, width), True, 2)
+    attended = jnp.sum(shares.astype(jnp.float32), axis=0)
+    own_rows = lax.dynamic_slice_in_dim(tokens, (2 * x + c) * slab, slab, 0)
+    mixed = (own_rows.astype(jnp.float32) + attended).astype(half_type)
+    normed_two = column_exchange(layer_norm(mixed).astype(half_type), False, 3).reshape(count, width)
+    hidden = []
+    for i in range(2):
+        gate_up = jnp.dot(normed_two, server_mid[i], preferred_element_type=jnp.float32)
+        hidden.append((jax.nn.silu(gate_up[:, :units]) * gate_up[:, units:]).astype(half_type))
+    hidden = jnp.concatenate(hidden, axis=1)
+    product = jnp.dot(hidden, server_down.reshape(2 * units, width), preferred_element_type=jnp.float32)
+    shares = column_exchange(product.astype(half_type).reshape(8, slab, width), True, 2)
+    return (mixed.astype(jnp.float32) + jnp.sum(shares.astype(jnp.float32), axis=0)).astype(half_type)
+
+
 def solution(mesh):
     in_specs = (
         P("dp", None),
@@ -136,6 +473,7 @@
         P("dp", "mp"),
     )
     out_specs = P(("dp", "mp"), None)
+    fits = mesh.shape["dp"] == 8 and mesh.shape["mp"] == 4
     return jax.shard_map(
-        on_device, mesh=mesh, in_specs=in_specs, out_specs=out_specs, check_vma=False
-    )
+        regrouped if fits else on_device, mesh=mesh, in_specs=in_specs, out_specs=out_specs, check_vma=False
+    )

time: 473 us -> 401 us (0.85)
  waiting for transfers between devices: 367 us -> 0 us
  Pallas kernels: 0 us -> 348 us
  starting transfers between devices: 35.1 us -> 0 us
  local copies, waits for them, and re-layouts: 3.89 us -> 22 us
  between operations: 13.8 us -> 0.41 us
  blocking collectives: 9.24 us -> 0 us
  matrix products: 22.8 us -> 15.4 us
    pallas_call x0 -> x5, Pallas kernels: none -> 348 us  [the longest x3 179 us: column_exchange(): pl.pallas_call(functools.partial(column_kernel, split), out_shape=jax.Sha...]
    all_gather x6 -> x0, waiting for transfers between devices: 298 us -> none  [the longest x1 94.3 us: on_device(): server_in = lax.all_gather(packed_in, 'dp', axis=0, tiled=True)]
    ppermute x4 -> x0, waiting for transfers between devices: 69.1 us -> none  [passed_along(): lax.ppermute(value, axis, [(source, source + steps) for source in range(i...]
    ppermute x4 -> x0, starting transfers between devices: 34.9 us -> none  [passed_along(): lax.ppermute(value, axis, [(source, source + steps) for source in range(i...]
    unnamed x16 -> x34, local copies, waits for them, and re-layouts: 0.65 us -> 11.2 us
    all_to_all x1 -> x0, blocking collectives: 9.24 us -> none  [on_device(): lax.all_to_all(own_out, 'mp', split_axis=0, concat_axis=1, tiled=True)]
    dot_general x14 -> x7, matrix products: 22.8 us -> 15.4 us  [the longest x1 7.24 us: regrouped(): jnp.dot(context, server_out.reshape(2 * HEAD, width), preferred_element_t...]
    slice x2 -> x5, local copies, waits for them, and re-layouts: 0.27 us -> 7.56 us  [the longest x1 4.74 us: regrouped(): pairs[:, 2:]]
  transfers between devices with their start and end apart: 10 -> 0, of which waited for: 10 -> 0; matrix products, arithmetic and copies ran while one was open for 4% -> 0% of each run, Pallas kernels for 0% -> 0%
where the time goes in v2:
time: 401 us
  Pallas kernels  348 us (87%)
  local copies, waits for them, and re-layouts  22 us (5%)
  other arithmetic  15.5 us (4%)
  matrix products  15.4 us (4%)
    pallas_call x3, Pallas kernels, column_exchange(): pl.pallas_call(functools.partial(column_kernel, split), out_shape=jax.Sha...  179 us
    pallas_call x1, Pallas kernels, regroup(): pl.pallas_call(regroup_kernel, out_shape=[jax.ShapeDtypeStruct(shape, hal...  141 us
    pallas_call x1, Pallas kernels, plane_gather(): pl.pallas_call(plane_kernel, out_shape=jax.ShapeDtypeStruct((4, *block.sh...  28.2 us
    unnamed x34, local copies, waits for them, and re-layouts  11.2 us

profile of v2, /device:TPU:9, one launch (start us, length us, event | category | flops | bytes accessed | tf_op | source)
XLA Modules:
  0.0 401.0 jit_solution(8820388197499505883)
XLA Ops:
  0.0 0.9 select_reduce_fusion
  0.9 1.2 convert_reduce_fusion.2
  2.1 1.3 fusion.11
  3.6 0.7 fusion.47
  4.6 0.5 multiply_cosine_fusion
  5.1 1.2 copy.30
  6.3 0.2 copy.33
  6.6 0.2 copy.34
  7.0 0.2 copy.35
  7.3 1.1 convert_element_type.95
  8.3 0.3 fusion.12.rows_ref
  8.7 1.4 copy.36
  10.1 0.2 copy.38
  10.3 1.4 copy.37
  11.7 0.2 copy.39
  12.1 1.1 copy-done.9
  13.2 1.9 compare_and_fusion
  15.1 140.6 %shard_map.91 = (bf16[2,8,256,384]{3,2,1,0:T(8,128)(2,1)S(1)}, bf16[2,8,256,512]{3,2,1,0:T(8,128)(2,1)S(1)}, bf16[2,128,2048]{2,1,0:T(8,128)(2,1)S(1)}, bf16[2,2...) custom-call(bf16[4,256,384]{2,1,0:T(8,128)(2,1)S(1)} %maximum_bitcast_fusion.1.in_ref, ...), custom_call_target="tpu_custom_call" | custom-call | tf_op jit(solution)/shard_map/pallas_call | solution.py:324
  155.7 1.9 copy-done
  157.7 1.4 copy-done.2
  159.1 0.4 fusion.58
  159.5 1.0 fusion.60
  160.5 1.0 fusion.61
  161.8 0.8 subtract_convert_fusion
  163.0 28.2 %shard_map.92 = bf16[4,512,512]{2,1,0:T(8,128)(2,1)S(1)} custom-call(bf16[512,512]{1,0:T(8,128)(2,1)S(1)} %pad_maximum_fusion.block_ref), custom_call_target="tpu_custom_call" | custom-call | tf_op jit(solution)/shard_map/pallas_call | solution.py:354
  191.2 2.1 reshape.291
  193.3 4.7 %fusion.59 = (bf16[2048,2,128]{2,1,0:T(2,128)(2,1)}, bf16[2048,2,128]{2,1,0:T(2,128)(2,1)S(1)}) fusion(bf16[2048,4,128]{2,1,0:T(4,128)(2,1)} %reshape.291), kind=kLoop, calls=%fused_computation.97 | loop fusion | bytes 4194304 | tf_op jit(solution)/shard_map/slice | solution.py:445
  198.0 2.4 fusion.57
  200.4 2.2 fusion
  202.6 2.5 fusion.1
  205.1 0.7 copy-done.4
  205.8 7.2 %bitcast_convert_fusion = bf16[512,2048]{1,0:T(8,128)(2,1)S(1)} fusion(bf16[2,128,2048]{2,1,0:T(8,128)(2,1)S(1)} %get-tuple-element.12, f32[2,512,2048]{2,1,0:T(8,128)} %copy-done.4, f32[2,512]{1,0:T(2,128)S(1)} %get-tuple-element.37, pred[512,2048]{1,0:T(8,128)(4,1)} %compare_and_fusion, bf16[2048,2,128]{2,1,0:T(2,128)(2,1)} %get-tuple-element.23, ...), kind=kOutput, calls=%fused_computation.5 | convolution fusion | flops 1083441152 | bytes 13639680 | tf_op jit(solution)/shard_map/dot_general | solution.py:447
  213.1 81.8 %shard_map.93 = bf16[8,64,2048]{2,1,0:T(8,128)(2,1)S(1)} custom-call(bf16[8,64,2048]{2,1,0:T(8,128)(2,1)S(1)} %bitcast.61), custom_call_target="tpu_custom_call" | custom-call | tf_op jit(solution)/shard_map/pallas_call | solution.py:385
  294.9 0.4 convert_reduce_fusion.1
  295.2 1.3 convert_reduce_fusion.3
  296.5 0.2 fusion.32
  296.8 0.2 fusion.33.block_ref
  296.9 48.6 %shard_map.94 = bf16[8,64,2048]{2,1,0:T(8,128)(2,1)S(1)} custom-call(bf16[64,2048]{1,0:T(8,128)(2,1)S(1)} %fusion.33.block_ref), custom_call_target="tpu_custom_call" | custom-call | tf_op jit(solution)/shard_map/pallas_call | solution.py:385
  345.5 1.3 fusion.63
  346.8 0.3 copy-done.7
  347.1 1.3 fusion.62
  348.4 0.2 fusion.36
  348.6 0.2 fusion.35
  348.8 1.2 copy-done.3
  350.0 1.3 convolution_convert_fusion
  351.3 48.6 %shard_map.95 = bf16[8,64,2048]{2,1,0:T(8,128)(2,1)S(1)} custom-call(bf16[8,64,2048]{2,1,0:T(8,128)(2,1)S(1)} %bitcast.62), custom_call_target="tpu_custom_call" | custom-call | tf_op jit(solution)/shard_map/pallas_call | solution.py:385
  399.9 0.4 convert_reduce_fusion
  400.3 0.8 fusion.34
  (46 shorter events, 1.6 us)
Async XLA Ops:
  0.0 6.8 %copy-start.11 = (f32[256,512]{1,0:T(8,128)S(1)}, f32[256,512]{1,0:T(8,128)}, u32[]{:S(2)}) copy-start(f32[256,512]{1,0:T(8,128)} %param.13) | copy-start | bytes 1572868
  0.0 6.5 %copy-start.10 = (f32[256,512]{1,0:T(8,128)S(1)}, f32[256,512]{1,0:T(8,128)}, u32[]{:S(2)}) copy-start(f32[256,512]{1,0:T(8,128)} %param.12) | copy-start | bytes 1572868
  6.6 1.7 copy-start.6
  11.9 1.2 copy-start.9
  155.7 1.9 copy-start
  157.7 1.4 copy-start.2
  193.3 4.7 %copy-start.1 = (bf16[2,8,256,512]{3,2,1,0:T(8,128)(2,1)S(1)}, bf16[2,8,256,512]{3,2,1,0:T(8,128)(2,1)}, u32[]{:S(2)}) copy-start(bf16[2,8,256,512]{3,2,1,0:T(8,128)(2,1)} %copy-done) | copy-start | bytes 12582916
  198.0 2.4 copy-start.5
  198.0 2.4 copy-start.12
  202.6 3.2 copy-start.4
  295.2 50.3 %copy-start.8 = (bf16[1,8,256,512]{3,2,1,0:T(8,128)(2,1)S(1)}, bf16[1,8,256,512]{3,2,1,0:T(8,128)(2,1)}, u32[]{:S(2)}) copy-start(bf16[1,8,256,512]{3,2,1,0:T(8,128)(2,1)} %get-tuple-element.20) | copy-start | bytes 6291460
  345.5 1.6 copy-start.7
  348.4 1.6 copy-start.3

commit v3 on v2

--- a/solution.py
+++ b/solution.py
@@ -163,11 +163,53 @@
     return [(k, f, device((z + k) % 4, y, x, (c + f) % 2)) for k, f in steps]
 
 
+class Spread:
+    def __init__(self, block_ref, all_ref, send, receive, core_send, core_recv, local_sem):
+        self.block, self.all, self.local_sem = block_ref, all_ref, local_sem
+        self.sems = send, receive, core_send, core_recv
+
+    def column(self, k):
+        z, y, x, c = place()
+        send, receive = self.sems[:2]
+        where = device((z + k) % 4, y, x, c)
+        return remote(self.block, self.all.at[2 * z + c], send.at[k], receive.at[k], where)
+
+    def core(self, k):
+        z, y, x, c = place()
+        send, receive = self.sems[2:]
+        slot = self.all.at[2 * ((z + 4 - k) % 4) + c]
+        source = self.block if k == 0 else slot
+        return remote(source, slot, send.at[k], receive.at[k], device(z, y, x, 1 - c))
+
+    def own(self):
+        z, y, x, c = place()
+        return pltpu.make_async_copy(self.block, self.all.at[2 * z + c], self.local_sem)
+
+    def start(self):
+        for k in (1, 3, 2):
+            self.column(k).start()
+        self.core(0).start()
+        self.own().start()
+
+    def relay(self):
+        for k in (1, 3, 2):
+            self.column(k).wait_recv()
+            self.core(k).start()
+
+    def finish(self):
+        self.own().wait()
+        for k in (1, 3, 2):
+            self.column(k).wait_send()
+        for k in range(4):
+            self.core(k).wait()
+
+
 def regroup_kernel(
     in_ref, mid_ref, out_ref, down_ref, rows_ref,
     in_all, mid_all, out_all, down_all, rows_all,
     column_send, column_recv, plane_send, plane_recv,
     part_send, part_recv, fan_send, fan_recv, local_sem,
+    rows_send, rows_recv, core_send, core_recv,
 ):
     z, y, x, c = place()
     own = 2 * z + y
@@ -182,16 +224,14 @@
     locals_ = []
     for i, (source, target) in enumerate(packs):
         locals_.append(pltpu.make_async_copy(source.at[z], target.at[x, own], local_sem.at[i]))
-    locals_.append(pltpu.make_async_copy(rows_ref, rows_all.at[z], local_sem.at[2]))
+    spread = Spread(rows_ref, rows_all, rows_send, rows_recv, core_send, core_recv, local_sem.at[2])
     for copy in locals_:
         copy.start()
     sends = []
 
     def column_copy(i, k):
         to = (z + k) % 4
-        source, target = packs[i] if i < 2 else (rows_ref, rows_all)
-        source = source.at[to] if i < 2 else source
-        target = target.at[x, own] if i < 2 else target.at[z]
+        source, target = packs[i][0].at[to], packs[i][1].at[x, own]
         return remote(source, target, column_send.at[i, k], column_recv.at[i, k], device(to, y, x, c))
 
     halves = ((out_ref, out_all), (down_ref, down_all))
@@ -214,10 +254,6 @@
         copy = column_copy(0, k)
         copy.start()
         sends.append(copy)
-    for k in (1, 3, 2):
-        copy = column_copy(2, k)
-        copy.start()
-        sends.append(copy)
     for i in range(2):
         for hf in range(2):
             source, target, send, receive = part_copy(i, hf)
@@ -238,8 +274,23 @@
         block = packs[i][1].at[x, 2 * ((z + 4 - k) % 4) + y]
         return [
             remote(block, block, plane_send.at[i, k, f], plane_recv.at[i, k, f], peer)
-            for f, peer in enumerate(plane)
+            for f, peer in enumerate(plane[:2])
         ]
+
+    def corner_copy(i, k, half):
+        zk = 2 * ((z + 4 - k) % 4)
+        rows = pl.ds(half * (packs[i][1].shape[2] // 2), packs[i][1].shape[2] // 2)
+        if half == 0:
+            block = packs[i][1].at[1 - x, zk + y, rows]
+        else:
+            block = packs[i][1].at[x, zk + 1 - y, rows]
+        return remote(block, block, plane_send.at[i, k, 2 + half], plane_recv.at[i, k, 2 + half], plane[1 - half])
+
+    def corner(i):
+        for k in (0, 1, 3, 2):
+            for half in range(2):
+                fan_copies(i, k)[half].wait_recv()
+                corner_copy(i, k, half).start()
 
     def part_block(i, p):
         return halves[i][1].at[p // 2, :, columns(2 * x + p % 2)]
@@ -261,6 +312,7 @@
                 copy.start()
 
     forward(0)
+    spread.start()
 
     @pl.when(hub)
     def _():
@@ -272,9 +324,10 @@
                     copy.start()
 
     forward(1)
-    locals_[2].wait()
-    for k in (1, 3, 2):
-        column_copy(2, k).wait_recv()
+    corner(0)
+    spread.relay()
+    corner(1)
+    spread.finish()
     for copy in sends:
         copy.wait_send()
     for i in range(2):
@@ -285,8 +338,9 @@
             def _():
                 remote(source, target, send, receive, device(2 * y + hf, y, x, z % 2)).wait_send()
         for k in range(4):
-            for copy in fan_copies(i, k):
-                copy.wait()
+            for half in range(2):
+                fan_copies(i, k)[half].wait_send()
+                corner_copy(i, k, half).wait()
 
     @pl.when(hub)
     def _():
@@ -318,7 +372,7 @@
         (2, 8, depth, cols_mid),
         (2, out.shape[1], 4 * out.shape[2]),
         (2, down.shape[1], 4 * down.shape[2]),
-        (4, *rows.shape),
+        (8, *rows.shape),
     )
     dma = pltpu.SemaphoreType.DMA
     return pl.pallas_call(
@@ -327,8 +381,9 @@
         in_specs=[any_spec()] * 5,
         out_specs=[any_spec()] * 5,
         scratch_shapes=[
-            dma((3, 4)), dma((3, 4)), dma((2, 4, 3)), dma((2, 4, 3)),
+            dma((2, 4)), dma((2, 4)), dma((2, 4, 4)), dma((2, 4, 4)),
             dma((2, 2)), dma((2, 4)), dma((2, 4, 3)), dma((2, 4, 3)), dma((3,)),
+            dma((4,)), dma((4,)), dma((4,)), dma((4,)),
         ],
         compiler_params=pltpu.CompilerParams(collective_id=0, has_side_effects=True, vmem_limit_bytes=1 << 20),
     )(*arrays)
@@ -361,35 +416,74 @@
     )(block)
 
 
-def column_kernel(split, block_ref, all_ref, send, receive, local_sem):
-    z, y, x, c = place()
-    peers = column_peers(z, y, x, c)
-    greet([peer for _, _, peer in peers])
-    target = all_ref.at[2 * z + c]
-    copies = []
-    for k, f, peer in peers:
-        source = block_ref.at[2 * ((z + k) % 4) + (c + f) % 2] if split else block_ref
-        copies.append(remote(source, target, send.at[k, f], receive.at[k, f], peer))
-    for copy in copies:
-        copy.start()
-    own = pltpu.make_async_copy(block_ref.at[2 * z + c] if split else block_ref, target, local_sem)
-    own.start()
-    own.wait()
-    for copy in copies:
-        copy.wait()
-
-
-def column_exchange(block, split, number):
+def near_peers(z, y, x, c):
+    return [device((z + k) % 4, y, x, c) for k in (1, 2, 3)] + [device(z, y, x, 1 - c)]
+
+
+def spread_kernel(block_ref, all_ref, send, receive, core_send, core_recv, local_sem):
+    greet(near_peers(*place()))
+    spread = Spread(block_ref, all_ref, send, receive, core_send, core_recv, local_sem)
+    spread.start()
+    spread.relay()
+    spread.finish()
+
+
+def column_gather(block):
     dma = pltpu.SemaphoreType.DMA
-    shape = block.shape if split else (8, *block.shape)
     return pl.pallas_call(
-        functools.partial(column_kernel, split),
-        out_shape=jax.ShapeDtypeStruct(shape, block.dtype),
+        spread_kernel,
+        out_shape=jax.ShapeDtypeStruct((8, *block.shape), block.dtype),
         in_specs=[any_spec()],
         out_specs=any_spec(),
-        scratch_shapes=[dma((4, 2)), dma((4, 2)), dma(())],
-        compiler_params=pltpu.CompilerParams(collective_id=number, has_side_effects=True, vmem_limit_bytes=1 << 20),
+        scratch_shapes=[dma((4,)), dma((4,)), dma((4,)), dma((4,)), dma(())],
+        compiler_params=pltpu.CompilerParams(collective_id=3, has_side_effects=True, vmem_limit_bytes=1 << 20),
     )(block)
+
+
+def column_sum_kernel(parts_ref, all_ref, given, summed, core_send, core_recv, send, receive):
+    z, y, x, c = place()
+    greet(near_peers(z, y, x, c))
+    order = (1, 3, 2, 0)
+
+    def core(k):
+        source = parts_ref.at[2 * ((z + k) % 4) + 1 - c]
+        return remote(source, given.at[k], core_send.at[k], core_recv.at[k], device(z, y, x, 1 - c))
+
+    def column(k):
+        where = device((z + k) % 4, y, x, c)
+        return remote(summed.at[k], all_ref.at[k], send.at[k], receive.at[k], where)
+
+    for k in order:
+        core(k).start()
+    for k in order:
+        core(k).wait_recv()
+        both = parts_ref[2 * ((z + k) % 4) + c].astype(jnp.float32) + given[k].astype(jnp.float32)
+        if k:
+            summed[k] = both.astype(summed.dtype)
+            column(k).start()
+        else:
+            all_ref[0] = both.astype(all_ref.dtype)
+    for k in order:
+        core(k).wait_send()
+        if k:
+            column(k).wait()
+
+
+def column_sum(parts):
+    dma = pltpu.SemaphoreType.DMA
+    half = (4, *parts.shape[1:])
+    vmem = pl.BlockSpec(memory_space=pltpu.VMEM)
+    return pl.pallas_call(
+        column_sum_kernel,
+        out_shape=jax.ShapeDtypeStruct(half, parts.dtype),
+        in_specs=[vmem],
+        out_specs=vmem,
+        scratch_shapes=[
+            pltpu.VMEM(half, parts.dtype), pltpu.VMEM(half, parts.dtype),
+            dma((4,)), dma((4,)), dma((4,)), dma((4,)),
+        ],
+        compiler_params=pltpu.CompilerParams(collective_id=2, has_side_effects=True, vmem_limit_bytes=24 << 20),
+    )(parts)
 
 
 def prompt_at(where, lengths):
@@ -414,8 +508,8 @@
     packed_mid = jnp.concatenate([pieces(w) for w in (w_gate, w_up)], axis=2).transpose(1, 0, 2)
     out = w_out.astype(half_type).reshape(2, -1, narrow)
     down = w_down.astype(half_type).reshape(2, -1, narrow)
-    chip_rows = lax.dynamic_slice_in_dim(tokens, x * 2 * slab, 2 * slab, 0)
-    normed = layer_norm(chip_rows).astype(half_type)
+    own_rows = lax.dynamic_slice_in_dim(tokens, (2 * x + c) * slab, slab, 0)
+    normed = layer_norm(own_rows).astype(half_type)
     server_in, server_mid, server_out, server_down, normed = regroup(packed_in, packed_mid, out, down, normed)
     count = 8 * slab
     normed = normed.reshape(count, width)
@@ -445,18 +539,17 @@
     accum = jnp.einsum("hqk,khd->qhd", weights.astype(half_type), pairs[:, 2:], preferred_element_type=jnp.float32)
     context = (accum / total.T[:, :, None]).astype(half_type).reshape(count, 2 * HEAD)
     partial = jnp.dot(context, server_out.reshape(2 * HEAD, width), preferred_element_type=jnp.float32)
-    shares = column_exchange(partial.astype(half_type).reshape(8, slab, width), True, 2)
+    shares = column_sum(partial.astype(half_type).reshape(8, slab, width))
     attended = jnp.sum(shares.astype(jnp.float32), axis=0)
-    own_rows = lax.dynamic_slice_in_dim(tokens, (2 * x + c) * slab, slab, 0)
     mixed = (own_rows.astype(jnp.float32) + attended).astype(half_type)
-    normed_two = column_exchange(layer_norm(mixed).astype(half_type), False, 3).reshape(count, width)
+    normed_two = column_gather(layer_norm(mixed).astype(half_type)).reshape(count, width)
     hidden = []
     for i in range(2):
         gate_up = jnp.dot(normed_two, server_mid[i], preferred_element_type=jnp.float32)
         hidden.append((jax.nn.silu(gate_up[:, :units]) * gate_up[:, units:]).astype(half_type))
     hidden = jnp.concatenate(hidden, axis=1)
     product = jnp.dot(hidden, server_down.reshape(2 * units, width), preferred_element_type=jnp.float32)
-    shares = column_exchange(product.astype(half_type).reshape(8, slab, width), True, 2)
+    shares = column_sum(product.astype(half_type).reshape(8, slab, width))
     return (mixed.astype(jnp.float32) + jnp.sum(shares.astype(jnp.float32), axis=0)).astype(half_type)
 
 

time: 401 us -> 324 us (0.81); the launches traced: 401 us -> 319 us
  Pallas kernels: 348 us -> 267 us
    pallas_call x3, Pallas kernels: 179 us -> 127 us  [the longest x2 101 us: column_sum(): pl.pallas_call(column_sum_kernel, out_shape=jax.ShapeDtypeStruct(half, pa...]
    pallas_call x1, Pallas kernels: 141 us -> 124 us  [regroup(): pl.pallas_call(regroup_kernel, out_shape=[jax.ShapeDtypeStruct(shape, hal...]
    pallas_call x1, Pallas kernels: 28.2 us -> 15.6 us  [plane_gather(): pl.pallas_call(plane_kernel, out_shape=jax.ShapeDtypeStruct((4, *block.sh...]
    unnamed x34 -> x30, local copies, waits for them, and re-layouts: 11.2 us -> 11.1 us
where the time goes in v3:
time: 324 us; the launch traced here: 319 us
  Pallas kernels  267 us (82%)
  local copies, waits for them, and re-layouts  21.9 us (7%)
  matrix products  15.4 us (5%)
  other arithmetic  14.9 us (5%)
    pallas_call x1, Pallas kernels, regroup(): pl.pallas_call(regroup_kernel, out_shape=[jax.ShapeDtypeStruct(shape, hal...  124 us
    pallas_call x2, Pallas kernels, column_sum(): pl.pallas_call(column_sum_kernel, out_shape=jax.ShapeDtypeStruct(half, pa...  101 us
    pallas_call x1, Pallas kernels, column_gather(): pl.pallas_call(spread_kernel, out_shape=jax.ShapeDtypeStruct((8, *block.s...  25.8 us
    pallas_call x1, Pallas kernels, plane_gather(): pl.pallas_call(plane_kernel, out_shape=jax.ShapeDtypeStruct((4, *block.sh...  15.6 us
    unnamed x30, local copies, waits for them, and re-layouts  11.1 us
    dot_general x1, matrix products, regrouped(): jnp.dot(context, server_out.reshape(2 * HEAD, width), preferred_element_t...  7.24 us

profile of v3, /device:TPU:9, one launch (start us, length us, event | category | flops | bytes accessed | tf_op | source)
XLA Modules:
  0.0 319.1 jit_solution(12085071901456922773)
XLA Ops:
  0.0 0.8 select_reduce_fusion
  0.8 1.1 convert_reduce_fusion.3
  1.9 1.2 fusion.32
  3.3 0.7 fusion.48
  4.3 0.5 multiply_cosine_fusion
  4.9 1.1 fusion.33.rows_ref
  5.9 1.2 copy.30
  7.1 0.2 copy.33
  7.5 0.2 copy.34
  7.6 1.3 copy.32
  8.9 0.2 copy.35
  9.2 1.1 convert_element_type.93
  10.3 0.2 copy.36
  10.5 0.2 copy.38
  10.7 1.4 copy.37
  12.1 0.2 copy.39
  12.5 1.1 copy-done.9
  13.7 1.9 compare_and_fusion
  15.5 123.7 %shard_map.91 = (bf16[2,8,256,384]{3,2,1,0:T(8,128)(2,1)S(1)}, bf16[2,8,256,512]{3,2,1,0:T(8,128)(2,1)S(1)}, bf16[2,128,2048]{2,1,0:T(8,128)(2,1)S(1)}, bf16[2,2...) custom-call(bf16[4,256,384]{2,1,0:T(8,128)(2,1)S(1)} %maximum_bitcast_fusion.1.in_ref, ...), custom_call_target="tpu_custom_call" | custom-call | tf_op jit(solution)/shard_map/pallas_call | solution.py:378
  139.2 1.9 copy-done
  141.1 1.4 copy-done.2
  142.5 0.4 fusion.60
  143.0 1.0 fusion.62
  144.0 1.0 fusion.63
  145.3 0.2 subtract_convert_fusion
  145.8 15.6 %shard_map.92 = bf16[4,512,512]{2,1,0:T(8,128)(2,1)S(1)} custom-call(bf16[512,512]{1,0:T(8,128)(2,1)S(1)} %pad_maximum_fusion.block_ref), custom_call_target="tpu_custom_call" | custom-call | tf_op jit(solution)/shard_map/pallas_call | solution.py:409
  161.5 2.1 reshape.291
  163.5 4.7 %fusion.61 = (bf16[2048,2,128]{2,1,0:T(2,128)(2,1)}, bf16[2048,2,128]{2,1,0:T(2,128)(2,1)S(1)}) fusion(bf16[2048,4,128]{2,1,0:T(4,128)(2,1)} %reshape.291), kind=kLoop, calls=%fused_computation.98 | loop fusion | bytes 4194304 | tf_op jit(solution)/shard_map/slice | solution.py:539
  168.3 2.3 fusion.59
  170.6 2.2 fusion
  172.8 2.5 fusion.1
  175.4 0.7 copy-done.4
  176.1 7.2 %bitcast_convert_fusion = bf16[512,2048]{1,0:T(8,128)(2,1)S(1)} fusion(bf16[2,128,2048]{2,1,0:T(8,128)(2,1)S(1)} %get-tuple-element.12, f32[2,512,2048]{2,1,0:T(8,128)} %copy-done.4, f32[2,512]{1,0:T(2,128)S(1)} %get-tuple-element.37, pred[512,2048]{1,0:T(8,128)(4,1)} %compare_and_fusion, bf16[2048,2,128]{2,1,0:T(2,128)(2,1)} %get-tuple-element.23, ...), kind=kOutput, calls=%fused_computation.5 | convolution fusion | flops 1083441152 | bytes 13639680 | tf_op jit(solution)/shard_map/dot_general | solution.py:541
  183.3 72.2 %shard_map.93 = bf16[4,64,2048]{2,1,0:T(8,128)(2,1)S(1)} custom-call(bf16[8,64,2048]{2,1,0:T(8,128)(2,1)S(1)} %bitcast.59), custom_call_target="tpu_custom_call" | custom-call | tf_op jit(solution)/shard_map/pallas_call | solution.py:476
  255.5 0.2 convert_reduce_fusion.1
  255.7 1.3 convert_reduce_fusion.2
  257.0 0.2 fusion.30
  257.4 25.8 %shard_map.94 = bf16[8,64,2048]{2,1,0:T(8,128)(2,1)S(1)} custom-call(bf16[64,2048]{1,0:T(8,128)(2,1)S(1)} %fusion.31.block_ref), custom_call_target="tpu_custom_call" | custom-call | tf_op jit(solution)/shard_map/pallas_call | solution.py:433
  283.2 1.3 fusion.65
  284.5 0.3 copy-done.6
  284.8 1.3 fusion.64
  286.1 0.2 fusion.37
  286.3 0.2 fusion.36
  286.4 1.2 copy-done.3
  287.7 1.3 convolution_convert_fusion
  289.0 29.2 %shard_map.95 = bf16[4,64,2048]{2,1,0:T(8,128)(2,1)S(1)} custom-call(bf16[8,64,2048]{2,1,0:T(8,128)(2,1)S(1)} %bitcast.62), custom_call_target="tpu_custom_call" | custom-call | tf_op jit(solution)/shard_map/pallas_call | solution.py:476
  318.2 0.2 convert_reduce_fusion
  318.4 0.8 fusion.35
  (42 shorter events, 1.6 us)
Async XLA Ops:
  0.0 7.3 %copy-start.10 = (f32[256,512]{1,0:T(8,128)S(1)}, f32[256,512]{1,0:T(8,128)}, u32[]{:S(2)}) copy-start(f32[256,512]{1,0:T(8,128)} %param.12) | copy-start | bytes 1572868
  7.5 2.8 copy-start.8
  12.4 1.2 copy-start.9
  139.2 1.9 copy-start
  141.1 1.4 copy-start.2
  163.5 4.7 %copy-start.1 = (bf16[2,8,256,512]{3,2,1,0:T(8,128)(2,1)S(1)}, bf16[2,8,256,512]{3,2,1,0:T(8,128)(2,1)}, u32[]{:S(2)}) copy-start(bf16[2,8,256,512]{3,2,1,0:T(8,128)(2,1)} %copy-done) | copy-start | bytes 12582916
  168.3 2.4 copy-start.5
  172.8 3.2 %copy-start.4 = (f32[2,512,2048]{2,1,0:T(8,128)}, f32[2,512,2048]{2,1,0:T(8,128)S(1)}, u32[]{:S(2)}) copy-start(f32[2,512,2048]{2,1,0:T(8,128)S(1)} %get-tuple-element.38) | copy-start | bytes 25165828
  255.7 27.5 %copy-start.7 = (bf16[1,8,256,512]{3,2,1,0:T(8,128)(2,1)S(1)}, bf16[1,8,256,512]{3,2,1,0:T(8,128)(2,1)}, u32[]{:S(2)}) copy-start(bf16[1,8,256,512]{3,2,1,0:T(8,128)(2,1)} %get-tuple-element.20) | copy-start | bytes 6291460
  283.2 1.6 copy-start.6
  286.1 1.6 copy-start.3

commit v4 on v3

--- a/solution.py
+++ b/solution.py
@@ -223,7 +223,7 @@
     packs = ((in_ref, in_all), (mid_ref, mid_all))
     locals_ = []
     for i, (source, target) in enumerate(packs):
-        locals_.append(pltpu.make_async_copy(source.at[z], target.at[x, own], local_sem.at[i]))
+        locals_.append(pltpu.make_async_copy(source.at[z], target.at[x, own] if i == 0 else target.at[z], local_sem.at[i]))
     spread = Spread(rows_ref, rows_all, rows_send, rows_recv, core_send, core_recv, local_sem.at[2])
     for copy in locals_:
         copy.start()
@@ -231,7 +231,8 @@
 
     def column_copy(i, k):
         to = (z + k) % 4
-        source, target = packs[i][0].at[to], packs[i][1].at[x, own]
+        source = packs[i][0].at[to]
+        target = packs[i][1].at[x, own] if i == 0 else packs[i][1].at[z]
         return remote(source, target, column_send.at[i, k], column_recv.at[i, k], device(to, y, x, c))
 
     halves = ((out_ref, out_all), (down_ref, down_all))
@@ -323,10 +324,11 @@
                 for copy in part_fan(i, p):
                     copy.start()
 
-    forward(1)
     corner(0)
     spread.relay()
-    corner(1)
+    locals_[1].wait()
+    for k in (1, 3, 2):
+        column_copy(1, k).wait_recv()
     spread.finish()
     for copy in sends:
         copy.wait_send()
@@ -337,10 +339,10 @@
             @pl.when(jnp.logical_not(is_self(hf)))
             def _():
                 remote(source, target, send, receive, device(2 * y + hf, y, x, z % 2)).wait_send()
-        for k in range(4):
-            for half in range(2):
-                fan_copies(i, k)[half].wait_send()
-                corner_copy(i, k, half).wait()
+    for k in range(4):
+        for half in range(2):
+            fan_copies(0, k)[half].wait_send()
+            corner_copy(0, k, half).wait()
 
     @pl.when(hub)
     def _():
@@ -369,7 +371,7 @@
     cols_mid = packed_mid.shape[2]
     shapes = (
         (2, 8, depth, cols_in),
-        (2, 8, depth, cols_mid),
+        (4, depth, cols_mid),
         (2, out.shape[1], 4 * out.shape[2]),
         (2, down.shape[1], 4 * down.shape[2]),
         (8, *rows.shape),
@@ -420,24 +422,45 @@
     return [device((z + k) % 4, y, x, c) for k in (1, 2, 3)] + [device(z, y, x, 1 - c)]
 
 
-def spread_kernel(block_ref, all_ref, send, receive, core_send, core_recv, local_sem):
-    greet(near_peers(*place()))
+def spread_kernel(
+    block_ref, mid_ref, all_ref, mid_all,
+    send, receive, core_send, core_recv, local_sem, mid_send, mid_recv, mid_sem,
+):
+    z, y, x, c = place()
+    plane = plane_peers(z, y, x, c)
+    greet(near_peers(z, y, x, c) + plane)
+    own = [pltpu.make_async_copy(mid_ref.at[k], mid_all.at[x, k, y], mid_sem.at[k]) for k in range(4)]
+    copies = [
+        remote(mid_ref.at[k], mid_all.at[x, k, y], mid_send.at[k, f], mid_recv.at[k, f], peer)
+        for k in range(4)
+        for f, peer in enumerate(plane)
+    ]
     spread = Spread(block_ref, all_ref, send, receive, core_send, core_recv, local_sem)
     spread.start()
+    for copy in copies + own:
+        copy.start()
     spread.relay()
     spread.finish()
-
-
-def column_gather(block):
+    for copy in copies + own:
+        copy.wait()
+
+
+def column_gather(block, mid):
     dma = pltpu.SemaphoreType.DMA
     return pl.pallas_call(
         spread_kernel,
-        out_shape=jax.ShapeDtypeStruct((8, *block.shape), block.dtype),
-        in_specs=[any_spec()],
-        out_specs=any_spec(),
-        scratch_shapes=[dma((4,)), dma((4,)), dma((4,)), dma((4,)), dma(())],
+        out_shape=[
+            jax.ShapeDtypeStruct((8, *block.shape), block.dtype),
+            jax.ShapeDtypeStruct((2, 4, 2, *mid.shape[1:]), mid.dtype),
+        ],
+        in_specs=[any_spec()] * 2,
+        out_specs=[any_spec()] * 2,
+        scratch_shapes=[
+            dma((4,)), dma((4,)), dma((4,)), dma((4,)), dma(()),
+            dma((4, 3)), dma((4, 3)), dma((4,)),
+        ],
         compiler_params=pltpu.CompilerParams(collective_id=3, has_side_effects=True, vmem_limit_bytes=1 << 20),
-    )(block)
+    )(block, mid)
 
 
 def column_sum_kernel(parts_ref, all_ref, given, summed, core_send, core_recv, send, receive):
@@ -514,7 +537,6 @@
     count = 8 * slab
     normed = normed.reshape(count, width)
     server_in = server_in.reshape(2, width, 3 * HEAD)
-    server_mid = server_mid.reshape(2, width, 2 * units)
     where = (
         jnp.arange(4)[:, None] * (2 * rows) + jnp.arange(2 * slab)[None, :]
     ).reshape(-1)
@@ -542,7 +564,9 @@
     shares = column_sum(partial.astype(half_type).reshape(8, slab, width))
     attended = jnp.sum(shares.astype(jnp.float32), axis=0)
     mixed = (own_rows.astype(jnp.float32) + attended).astype(half_type)
-    normed_two = column_gather(layer_norm(mixed).astype(half_type)).reshape(count, width)
+    normed_two, server_mid = column_gather(layer_norm(mixed).astype(half_type), server_mid)
+    normed_two = normed_two.reshape(count, width)
+    server_mid = server_mid.reshape(2, width, 2 * units)
     hidden = []
     for i in range(2):
         gate_up = jnp.dot(normed_two, server_mid[i], preferred_element_type=jnp.float32)

time: 324 us -> 309 us (0.954)
  Pallas kernels: 267 us -> 255 us
  local copies, waits for them, and re-layouts: 21.9 us -> 17.2 us
    pallas_call x1, Pallas kernels: 25.8 us -> 50.4 us  [column_gather(): pl.pallas_call(spread_kernel, out_shape=[jax.ShapeDtypeStruct((8, *block....]
    pallas_call x1, Pallas kernels: 124 us -> 99.4 us  [regroup(): pl.pallas_call(regroup_kernel, out_shape=[jax.ShapeDtypeStruct(shape, hal...]
    pallas_call x2, Pallas kernels: 101 us -> 80.9 us  [column_sum(): pl.pallas_call(column_sum_kernel, out_shape=jax.ShapeDtypeStruct(half, pa...]
    pallas_call x1, Pallas kernels: 15.6 us -> 24.7 us  [plane_gather(): pl.pallas_call(plane_kernel, out_shape=jax.ShapeDtypeStruct((4, *block.sh...]
    unnamed x30 -> x36, local copies, waits for them, and re-layouts: 11.1 us -> 8.33 us
where the time goes in v4:
time: 309 us; the launch traced here: 305 us
  Pallas kernels  255 us (83%)
  local copies, waits for them, and re-layouts  17.2 us (6%)
  other arithmetic  16.7 us (5%)
  matrix products  15.5 us (5%)
    pallas_call x1, Pallas kernels, regroup(): pl.pallas_call(regroup_kernel, out_shape=[jax.ShapeDtypeStruct(shape, hal...  99.4 us
    pallas_call x2, Pallas kernels, column_sum(): pl.pallas_call(column_sum_kernel, out_shape=jax.ShapeDtypeStruct(half, pa...  80.9 us
    pallas_call x1, Pallas kernels, column_gather(): pl.pallas_call(spread_kernel, out_shape=[jax.ShapeDtypeStruct((8, *block....  50.4 us
    pallas_call x1, Pallas kernels, plane_gather(): pl.pallas_call(plane_kernel, out_shape=jax.ShapeDtypeStruct((4, *block.sh...  24.7 us
    unnamed x36, local copies, waits for them, and re-layouts  8.33 us
    dot_general x1, matrix products, regrouped(): jnp.dot(context, server_out.reshape(2 * HEAD, width), preferred_element_t...  7.54 us

profile of v4, /device:TPU:9, one launch (start us, length us, event | category | flops | bytes accessed | tf_op | source)
XLA Modules:
  0.0 305.2 jit_solution(9155000344009334417)
XLA Ops:
  0.0 0.9 select_reduce_fusion
  0.9 1.1 convert_reduce_fusion.3
  2.0 1.2 fusion.32
  3.4 1.3 fusion.48
  4.9 1.2 multiply_cosine_fusion
  6.1 1.1 fusion.33.rows_ref
  7.2 1.2 copy.30
  8.4 0.2 copy.33
  8.7 0.2 copy.34
  9.1 0.2 copy.35
  9.3 1.1 convert_element_type.93
  10.4 0.2 copy.36
  10.6 0.2 copy.38
  10.9 1.4 copy.37
  12.3 0.2 copy.39
  12.6 1.1 copy-done.6
  13.8 1.9 compare_and_fusion
  15.7 99.4 %shard_map.91 = (bf16[2,8,256,384]{3,2,1,0:T(8,128)(2,1)S(1)}, bf16[4,256,512]{2,1,0:T(8,128)(2,1)S(1)}, bf16[2,128,2048]{2,1,0:T(8,128)(2,1)S(1)}, bf16[2,256,2...) custom-call(bf16[4,256,384]{2,1,0:T(8,128)(2,1)S(1)} %maximum_bitcast_fusion.1.in_ref, ...), custom_call_target="tpu_custom_call" | custom-call | tf_op jit(solution)/shard_map/pallas_call | solution.py:380
  115.1 1.4 copy-done
  116.5 1.0 copy-done.2
  117.5 0.4 fusion.60
  117.9 1.0 fusion.62
  119.0 1.0 fusion.63
  120.3 0.6 copy-done.7
  120.9 0.8 subtract_convert_fusion
  121.9 0.1 copy.49
  122.1 24.7 %shard_map.92 = bf16[4,512,512]{2,1,0:T(8,128)(2,1)S(1)} custom-call(bf16[512,512]{1,0:T(8,128)(2,1)S(1)} %pad_maximum_fusion.block_ref), custom_call_target="tpu_custom_call" | custom-call | tf_op jit(solution)/shard_map/pallas_call | solution.py:411
  146.7 2.1 reshape.291
  148.8 4.8 %fusion.61 = (bf16[2048,2,128]{2,1,0:T(2,128)(2,1)}, bf16[2048,2,128]{2,1,0:T(2,128)(2,1)S(1)}) fusion(bf16[2048,4,128]{2,1,0:T(4,128)(2,1)} %reshape.291), kind=kLoop, calls=%fused_computation.98 | loop fusion | bytes 4194304 | tf_op jit(solution)/shard_map/slice | solution.py:561
  153.7 2.1 fusion
  155.8 2.5 fusion.1
  158.3 0.8 copy-done.3
  159.0 7.5 %bitcast_convert_fusion = bf16[512,2048]{1,0:T(8,128)(2,1)S(1)} fusion(bf16[2,128,2048]{2,1,0:T(8,128)(2,1)} %copy-done.2, f32[2,512,2048]{2,1,0:T(8,128)} %copy-done.3, f32[2,512]{1,0:T(2,128)S(1)} %get-tuple-element.41, pred[512,2048]{1,0:T(8,128)(4,1)} %compare_and_fusion, bf16[2048,2,128]{2,1,0:T(2,128)(2,1)} %get-tuple-element.27, f32[512,2]{0,1:T(2,128)S(1)} %bitcast.80), kind=kOutput, calls=%fused_computation.5 | convolution fusion | flops 1083441152 | bytes 13639680 | tf_op jit(solution)/shard_map/dot_general | solution.py:563
  166.6 53.7 %shard_map.93 = bf16[4,64,2048]{2,1,0:T(8,128)(2,1)S(1)} custom-call(bf16[8,64,2048]{2,1,0:T(8,128)(2,1)S(1)} %bitcast.59), custom_call_target="tpu_custom_call" | custom-call | tf_op jit(solution)/shard_map/pallas_call | solution.py:499
  220.3 0.2 convert_reduce_fusion.1
  220.5 1.1 convert_reduce_fusion.2
  221.6 0.2 fusion.30
  221.9 0.2 fusion.31.block_ref
  222.0 50.4 %shard_map.94 = (bf16[8,64,2048]{2,1,0:T(8,128)(2,1)S(1)}, bf16[2,4,2,256,512]{4,3,2,1,0:T(8,128)(2,1)S(1)}) custom-call(bf16[64,2048]{1,0:T(8,128)(2,1)S(1)} %fusion.31.block_ref, bf16[4,256,512]{2,1,0:T(8,128)(2,1)S(1)} %get-tuple-element.15.mid_ref), custom_call_target="tpu_custom_call" | custom-call | tf_op jit(solution)/shard_map/pallas_call | solution.py:450
  272.4 0.4 fusion.59
  272.8 1.3 fusion.64
  274.1 0.2 fusion.37
  274.3 1.3 fusion.65
  275.6 0.2 fusion.36
  275.9 1.3 convolution_convert_fusion
  277.1 27.1 %shard_map.95 = bf16[4,64,2048]{2,1,0:T(8,128)(2,1)S(1)} custom-call(bf16[8,64,2048]{2,1,0:T(8,128)(2,1)S(1)} %bitcast.60), custom_call_target="tpu_custom_call" | custom-call | tf_op jit(solution)/shard_map/pallas_call | solution.py:499
  304.3 0.2 convert_reduce_fusion
  304.4 0.8 fusion.35
  (48 shorter events, 1.5 us)
Async XLA Ops:
  0.0 8.9 %copy-start.9 = (f32[256,512]{1,0:T(8,128)S(1)}, f32[256,512]{1,0:T(8,128)}, u32[]{:S(2)}) copy-start(f32[256,512]{1,0:T(8,128)} %param.13) | copy-start | bytes 1572868
  0.0 8.6 %copy-start.8 = (f32[256,512]{1,0:T(8,128)S(1)}, f32[256,512]{1,0:T(8,128)}, u32[]{:S(2)}) copy-start(f32[256,512]{1,0:T(8,128)} %param.12) | copy-start | bytes 1572868
  3.3 1.4 copy-start.11
  8.7 1.7 copy-start.5
  12.5 1.2 copy-start.6
  12.5 1.3 copy-start.12
  12.5 1.3 copy-start.13
  115.1 1.4 copy-start
  116.5 1.0 copy-start.2
  120.0 0.9 copy-start.7
  148.8 4.8 %copy-start.4 = (pred[512,2048]{1,0:T(8,128)(4,1)S(1)}, pred[512,2048]{1,0:T(8,128)(4,1)}, u32[]{:S(2)}) copy-start(pred[512,2048]{1,0:T(8,128)(4,1)} %compare_and_fusion) | copy-start | bytes 3145732
  148.8 4.8 %copy-start.10 = (bf16[512,2,64]{0,2,1:T(8,128)(2,1)S(1)}, bf16[512,2,64]{0,2,1:T(8,128)(2,1)}, u32[]{:S(2)}) copy-start(bf16[512,2,64]{0,2,1:T(8,128)(2,1)} %get-tuple-element.30) | copy-start | bytes 393220
  155.8 3.2 %copy-start.3 = (f32[2,512,2048]{2,1,0:T(8,128)}, f32[2,512,2048]{2,1,0:T(8,128)S(1)}, u32[]{:S(2)}) copy-start(f32[2,512,2048]{2,1,0:T(8,128)S(1)} %get-tuple-element.42) | copy-start | bytes 25165828
  274.3 1.6 copy-start.1
